TPU v7x, 128 devices: a whole 4x4x4 slice. The times are simulated.
128 devices in a mesh: cache: 32 (over y, x, core), psg: 4 (over z).
Axes of the slice: x: 4, y: 4, z: 4, core: 2. Of those that a mesh axis runs over, the one named last changes fastest.
Arguments:
- question_ids: int32 [32, 16], P('cache'), may hold values from 0 to 32127
- answer_ids: int32 [32, 32], P('cache'), may hold values from 0 to 32127
- owner: int32 [32, 32, 1], P('cache', 'psg'), may hold values from 0 to 31; in each aligned block of 32 rows (0 to 31, 32 to 63, ..., all dimensions but the last counted through in order) at most 2 rows name the same one
- slot: int32 [32, 32], P('cache', 'psg'), may hold values from 0 to 31
- passage_score: float32 [32, 32], P('cache', 'psg'), may hold values from -4 to 304
- memory: bfloat16 [1024, 16, 4096], P('cache', None, 'psg'), may hold values from -64 to 64
- embedding: bfloat16 [32128, 4096], P('cache', 'psg'), may hold values from -6 to 6
- live_gain: float32 [4096], replicated, may hold values from 0.1 to 1.9
- live_qkv: bfloat16 [4096, 3, 2048], P(None, None, 'psg'), may hold values from -0.09375 to 0.09375
- rel_bias: float32 [32, 32], P('psg'), may hold values from -6 to 306
- live_out: bfloat16 [2048, 4096], P('psg'), may hold values from -0.375 to 0.375
- enc_gain: float32 [4096], replicated, may hold values from 0.1 to 1.9
- cross_kv: bfloat16 [4096, 2, 2048], P(None, None, 'psg'), may hold values from -0.09375 to 0.09375
- dec_gain: float32 [4096], replicated, may hold values from 0.1 to 1.9
- cross_query: bfloat16 [4096, 2048], P(None, 'psg'), may hold values from -0.09375 to 0.09375
- cross_out: bfloat16 [2048, 4096], P('psg'), may hold values from -0.375 to 0.375
Outputs:
- encoded: bfloat16 [32, 32, 32, 4096], P('cache', 'psg')
- decoded: bfloat16 [32, 32, 4096], P('cache', None, 'psg')
Inputs may be any that keep to these rules, and one draw needn't show every extreme that they name: Among the 32 passages of one question at most 2 have the same owner, and in some question an owner has exactly 2.
All inputs are finite; a program needn't handle non-finite values.
Results may differ from a plain program's by a relative error of at most 0.025.
Values may be sent and summed in bfloat16 or wider, within the bound.
A program may use at most 192 MiB of HBM per device.

v0:
```python
import jax
import jax.numpy as jnp
import numpy as np
from jax import lax
from jax.sharding import PartitionSpec as P

HEAD = 64


EPSILON = 1e-06


def joined(part, axis, combine):
    gathered = jax.tree.map(lambda a: lax.all_gather(a, axis), part)

    def take(source):
        return jax.tree.map(lambda a: lax.dynamic_index_in_dim(a, source, 0, False), gathered)

    return lax.fori_loop(
        1, lax.axis_size(axis), lambda source, state: combine(state, take(source)), take(0)
    )


def bucket_table(length, bucket_count):
    positions = np.arange(length)
    relative = positions[None, :] - positions[:, None]
    halfway = bucket_count // 2
    exact_span = halfway // 2
    upper_side = (relative > 0).astype(np.int64) * halfway
    distance = np.abs(relative)
    log_bucket = exact_span + (
        np.log(np.maximum(distance, 1) / exact_span)
        / np.log(128.0 / exact_span)
        * (halfway - exact_span)
    ).astype(np.int64)
    log_bucket = np.minimum(log_bucket, halfway - 1)
    return upper_side + np.where(distance < exact_span, distance, log_bucket)


def position_bias(bias_table, length):
    bucket_count = bias_table.shape[1]
    buckets = bucket_table(length, bucket_count).reshape(-1)
    onehot = (buckets[None, :] == np.arange(bucket_count)[:, None]).astype(np.float32)
    spread = jnp.dot(
        bias_table, jnp.asarray(onehot, dtype=bias_table.dtype), precision=lax.Precision.HIGHEST
    )
    return spread.reshape(bias_table.shape[0], length, length)


def norm_project(rows_in, gain_vector, weights):
    wide = rows_in.astype(jnp.float32)
    inverse = lax.rsqrt(jnp.mean(wide * wide, axis=-1, keepdims=True) + EPSILON)
    scaled = (wide * gain_vector).astype(jnp.bfloat16)
    projected = jnp.dot(scaled, weights, preferred_element_type=jnp.float32)
    return (projected * inverse).astype(jnp.bfloat16)


def softmax_rows(scores):
    maximum = jnp.max(scores, axis=-1, keepdims=True)
    exponents = jnp.exp(scores - maximum)
    return (exponents / jnp.sum(exponents, axis=-1, keepdims=True)).astype(jnp.bfloat16)


def make_adder(gain_vector, weights, own_start, own_count, piece_rows):
    amount = piece_rows.shape[-1]
    wide = piece_rows.astype(jnp.float32)
    scaled = (wide * gain_vector).astype(jnp.bfloat16).reshape(-1, amount)
    totals = jnp.dot(scaled, weights, preferred_element_type=jnp.float32)
    squares = jnp.sum(wide * wide, axis=-1).reshape(-1)
    own_piece = lax.dynamic_slice_in_dim(piece_rows, own_start, own_count, 0)
    return (totals, squares, own_piece)


def finish_fold(totals, squares, model_width):
    inverse = lax.rsqrt(squares / model_width + EPSILON)
    return (totals * inverse[:, None]).astype(jnp.bfloat16)


def combine_parts(first_part, second_part):
    max_first, sum_first, value_first = first_part
    max_second, sum_second, value_second = second_part
    maximum = jnp.maximum(max_first, max_second)
    scale_first = jnp.exp(max_first - maximum)
    scale_second = jnp.exp(max_second - maximum)
    row_sums = sum_first * scale_first + sum_second * scale_second
    weighted = value_first * scale_first[..., None] + value_second * scale_second[..., None]
    return (maximum, row_sums, weighted)


def shards(
    question_ids,
    answer_ids,
    owner,
    slot,
    passage_score,
    memory,
    embedding,
    live_gain,
    live_qkv,
    rel_bias,
    live_out,
    enc_gain,
    cross_kv,
    dec_gain,
    cross_query,
    cross_out,
):
    cache_size = lax.axis_size("cache")
    psg_count = lax.axis_size("psg")
    own_index = lax.axis_index("psg")
    model_width = live_gain.shape[0]
    slice_width = memory.shape[2]
    passage_len = memory.shape[1]
    question_len = question_ids.shape[1]
    seq_len = passage_len + question_len
    head_size = HEAD
    score_scale = head_size ** (-0.5)
    heads_live = rel_bias.shape[0]
    live_cols = live_out.shape[0]
    cross_cols = cross_out.shape[0]
    own_count = owner.shape[1]
    own_start = own_index * own_count
    question_all, answer_all = (
        lax.all_gather(question_ids, "cache", axis=0, tiled=True),
        lax.all_gather(answer_ids, "cache", axis=0, tiled=True),
    )
    token_all = jnp.concatenate([question_all, answer_all], axis=1)
    vocab_rows = embedding.shape[0]
    vocab_first = lax.axis_index("cache") * vocab_rows
    picked = token_all - vocab_first
    onehot = (picked[:, :, None] == jnp.arange(vocab_rows, dtype=jnp.int32)[None, None, :]).astype(
        jnp.bfloat16
    )
    token_slice = lax.psum_scatter(
        jnp.einsum("qtv,vf->qtf", onehot, embedding, preferred_element_type=jnp.float32).astype(
            jnp.bfloat16
        ),
        "cache",
        scatter_dimension=0,
        tiled=True,
    )
    token_full = lax.all_gather(token_slice, "psg", axis=2, tiled=True)
    question_full = token_full[0, :question_len]
    answer_full = token_full[0, question_len:]
    owner_all, slot_all = (
        lax.all_gather(owner, "psg", axis=1, tiled=True),
        lax.all_gather(slot, "psg", axis=1, tiled=True),
    )
    owner_list = owner_all[0, :, 0]
    slot_list = slot_all[0]
    total_psg = owner_list.shape[0]
    capacity = 2 * total_psg // cache_size
    positions = jnp.arange(total_psg)
    same_owner = owner_list[:, None] == owner_list[None, :]
    order_rank = jnp.sum(same_owner & (positions[None, :] < positions[:, None]), axis=1)
    owner_hit = owner_list[None, :] == jnp.arange(cache_size)[:, None]
    rank_hit = order_rank[None, :] == jnp.arange(capacity)[:, None]
    requests = jnp.sum(
        jnp.where(owner_hit[:, None, :] & rank_hit[None, :, :], slot_list[None, None, :], 0), axis=2
    )
    asked_slots = lax.all_to_all(requests, "cache", split_axis=0, concat_axis=0, tiled=True)
    looked_up = jnp.take(memory, asked_slots.reshape(-1), axis=0)
    looked_up = looked_up.reshape(asked_slots.shape + memory.shape[1:])
    fetched = lax.all_to_all(looked_up, "cache", split_axis=0, concat_axis=0, tiled=True)
    memory_slices = jnp.take(
        fetched.reshape((-1,) + memory.shape[1:]), owner_list * capacity + order_rank, axis=0
    )
    qkv_weights = live_qkv.reshape(model_width, 3 * live_cols)
    mem_totals, mem_squares, own_memory = make_adder(
        live_gain,
        qkv_weights,
        own_start,
        own_count,
        lax.all_gather(memory_slices, "psg", axis=2, tiled=True),
    )
    mem_proj = finish_fold(mem_totals, mem_squares, model_width).reshape(
        total_psg, passage_len, 3 * live_cols
    )
    question_proj = norm_project(question_full, live_gain, qkv_weights)
    projections = jnp.concatenate(
        [mem_proj, jnp.broadcast_to(question_proj[None], (total_psg, question_len, 3 * live_cols))],
        axis=1,
    )
    projections = projections.reshape(total_psg, seq_len, 3, heads_live, head_size)
    position = position_bias(rel_bias, seq_len)
    scores = (
        jnp.einsum(
            "pqhd,pkhd->phqk",
            projections[:, :, 0],
            projections[:, :, 1],
            preferred_element_type=jnp.float32,
        )
        * score_scale
        + position[None]
    )
    weights = softmax_rows(scores)
    context = (
        jnp.einsum(
            "phqk,pkhd->pqhd", weights, projections[:, :, 2], preferred_element_type=jnp.float32
        )
        .astype(jnp.bfloat16)
        .reshape(total_psg * seq_len, live_cols)
    )
    kv_weights = cross_kv.reshape(model_width, 2 * cross_cols)
    attended = lax.psum_scatter(
        jnp.dot(context, live_out, preferred_element_type=jnp.float32).astype(jnp.bfloat16),
        "psg",
        scatter_dimension=0,
        tiled=True,
    ).astype(jnp.float32)
    own_input = jnp.concatenate(
        [own_memory, jnp.broadcast_to(question_full[None], (own_count, question_len, model_width))],
        axis=1,
    ).reshape(own_count * seq_len, model_width)
    encoded_rows = (own_input.astype(jnp.float32) + attended).astype(jnp.bfloat16)
    keys_values = norm_project(
        lax.all_gather(encoded_rows, "psg", axis=0, tiled=True), enc_gain, kv_weights
    )
    keys_cross = keys_values[:, :cross_cols]
    values_cross = keys_values[:, cross_cols:]
    dec_queries = norm_project(answer_full, dec_gain, cross_query)
    answer_len = answer_full.shape[0]
    key_block = keys_cross.reshape(psg_count, own_count * seq_len, cross_cols)
    value_block = values_cross.reshape(psg_count, own_count * seq_len, cross_cols)
    own_keys, own_values = (
        lax.all_to_all(key_block, "psg", split_axis=0, concat_axis=2, tiled=True),
        lax.all_to_all(value_block, "psg", split_axis=0, concat_axis=2, tiled=True),
    )
    query_all = lax.all_gather(dec_queries, "psg", axis=1, tiled=True)
    heads_all = query_all.shape[1] // head_size
    own_bias = jnp.repeat(passage_score[0], seq_len)
    scores_cross = (
        jnp.einsum(
            "qhd,khd->qhk",
            query_all.reshape(answer_len, heads_all, head_size),
            own_keys.reshape(own_count * seq_len, heads_all, head_size),
            preferred_element_type=jnp.float32,
        )
        * score_scale
        + own_bias
    )
    maximum = jnp.max(scores_cross, axis=-1)
    exponents = jnp.exp(scores_cross - maximum[..., None])
    row_sums = jnp.sum(exponents, axis=-1)
    weighted = jnp.einsum(
        "qhk,khd->qhd",
        exponents.astype(jnp.bfloat16),
        own_values.reshape(own_count * seq_len, heads_all, head_size),
        preferred_element_type=jnp.float32,
    )
    maximum, row_sums, weighted = joined((maximum, row_sums, weighted), "psg", combine_parts)
    merged = (
        (weighted / row_sums[..., None])
        .astype(jnp.bfloat16)
        .reshape(answer_len, heads_all * head_size)
    )
    cross_context = lax.dynamic_slice_in_dim(merged, own_index * cross_cols, cross_cols, 1)
    decoded = lax.psum_scatter(
        jnp.dot(cross_context, cross_out, preferred_element_type=jnp.float32).astype(jnp.bfloat16),
        "psg",
        scatter_dimension=1,
        tiled=True,
    )
    return (
        encoded_rows.reshape(1, own_count, seq_len, model_width),
        decoded.reshape(1, answer_len, slice_width),
    )


def solution(mesh):
    return jax.shard_map(
        shards,
        mesh=mesh,
        in_specs=(
            P("cache", None),
            P("cache", None),
            P("cache", "psg", None),
            P("cache", "psg"),
            P("cache", "psg"),
            P("cache", None, "psg"),
            P("cache", "psg"),
            P(),
            P(None, None, "psg"),
            P("psg", None),
            P("psg", None),
            P(),
            P(None, None, "psg"),
            P(),
            P(None, "psg"),
            P("psg", None),
        ),
        out_specs=(P("cache", "psg", None, None), P("cache", None, "psg")),
        check_vma=False,
    )
```

profile of v0, /device:TPU:1, one launch (start us, length us, event | category | flops | bytes accessed | tf_op | source)
XLA Modules:
  0.0 521.5 jit_solution(14778956911780686364)
XLA Ops:
  8.1 23.2 %all-gather.3 = s32[32,1,16]{2,1,0:T(1,128)S(1)} all-gather(s32[1,1,16]{2,1,0:T(1,128)} %bitcast.134), channel_id=1, replica_groups=mesh['cache'=32,'psg'=4] {'cache'}, dimensions={0}, use_global_device_ids=true | all-gather | bytes 2112 | tf_op jit(solution)/shard_map/all_gather | solution.py:124
  31.3 20.2 %all-gather.4 = s32[32,1,32]{2,1,0:T(1,128)S(1)} all-gather(s32[1,1,32]{2,1,0:T(1,128)} %bitcast.135), channel_id=1, replica_groups=mesh['cache'=32,'psg'=4] {'cache'}, dimensions={0}, use_global_device_ids=true | all-gather | bytes 4224 | tf_op jit(solution)/shard_map/all_gather | solution.py:125
  51.6 4.8 fusion.17
  57.9 7.7 %all-reduce.2 = (s32[32]{0:T(128)S(1)}, s32[32]{0:T(128)S(1)}) all-reduce(s32[32]{0:T(128)S(1)} %bitcast_dynamic-update-slice_fusion, s32[32]{0:T(128)S(1)} %bitcast_dynamic-update-slice_fusion.1), channel_id=1, replica_groups=mesh['cache'=32,'psg'=4] {'psg'}, use_global_device_ids=true, to_apply=%add.1 | all-reduce | flops 64 | bytes 512
  66.1 14.2 %all_to_all.44 = s32[32,1,2]{2,1,0:T(1,128)S(1)} all-to-all(s32[32,1,2]{2,1,0:T(1,128)S(1)} %copy.79), channel_id=1, replica_groups=mesh['cache'=32,'psg'=4] {'cache'}, dimensions={0} | all-to-all | bytes 512 | tf_op jit(solution)/shard_map/all_to_all | solution.py:161
  81.8 2.0 gather_fusion
  83.8 3.2 broadcast_select_fusion
  87.0 5.0 all-to-all-start.1
  92.1 34.0 %all-to-all-done.1 = bf16[32,2,16,1024]{3,2,1,0:T(8,128)(2,1)} async-done(((bf16[32,2,16,1024]{3,2,1,0:T(8,128)(2,1)}), bf16[32,2,16,1024]{3,2,1,0:T(8,128)(2,1)}, u32[]{:S(2)}, u32[]{:S(2)}) %all-to-all-start.1) | async-done | bytes 2097184 | tf_op jit(solution)/shard_map/all_to_all | solution.py:164
  126.1 2.2 gather_fusion.1
  128.3 1.1 broadcast_select_fusion.1
  129.6 17.1 %copy.82 = bf16[4096,3,512]{0,2,1:T(8,128)(2,1)} copy(bf16[4096,3,512]{2,0,1:T(8,128)(2,1)} %param.27) | data formatting | bytes 25165824 | tf_op args[8]
  147.1 12.9 %all_gather.47 = bf16[1,48,4096]{2,1,0:T(8,128)(2,1)S(1)} all-gather(bf16[1,48,1024]{2,1,0:T(8,128)(2,1)} %reduce-scatter.4.cloned.1.call-done), channel_id=1, replica_groups=mesh['cache'=32,'psg'=4] {'psg'}, dimensions={2}, use_global_device_ids=true | all-gather | bytes 491520 | tf_op jit(solution)/shard_map/all_gather | solution.py:142
  160.1 8.0 %fusion.20 = bf16[16,1536]{1,0:T(8,128)(2,1)S(1)} fusion(bf16[4096,1536]{0,1:T(8,128)(2,1)} %bitcast.115, f32[4096]{0:T(1024)S(1)} %copy-done.5, bf16[1,48,4096]{2,1,0:T(8,128)(2,1)S(1)} %all_gather.47, f32[16]{0:T(128)S(1)} %add_rsqrt_fusion.3), kind=kOutput, calls=%fused_computation.43 | convolution fusion | flops 201572352 | bytes 12780032 | tf_op jit(solution)/shard_map/dot_general | solution.py:54
  168.3 9.1 %all-gather.9.cloned.1.call-done = bf16[32,16,4096]{2,1,0:T(8,128)(2,1)} async-done(((bf16[32,16,1024]{2,1,0:T(8,128)(2,1)}), bf16[32,16,4096]{2,1,0:T(8,128)(2,1)}) %all-gather.9.cloned.1.call-update) | async-done | bytes 4194320 | tf_op jit(solution)/shard_map/all_gather | solution.py:174
  177.4 5.7 %fusion.8 = (f32[32,16]{1,0:T(8,128)S(1)}, bf16[32,16,4096]{2,1,0:T(8,128)(2,1)}) fusion(bf16[32,16,4096]{2,1,0:T(8,128)(2,1)} %all-gather.9.cloned.1.call-done, f32[4096]{0:T(1024)S(1)} %copy-done.5), kind=kLoop, calls=%fused_computation.22 | loop fusion | flops 10485248 | bytes 8407040 | tf_op jit(solution)/shard_map/reduce_sum | solution.py:69
  183.2 11.1 %fusion.16 = bf16[512,1536]{1,0:T(8,128)(2,1)S(1)} fusion(bf16[512,4096]{1,0:T(8,128)(2,1)} %bitcast.122, bf16[4096,1536]{0,1:T(8,128)(2,1)} %bitcast.116, f32[512]{0:T(512)S(1)} %rsqrt.35), kind=kOutput, calls=%fused_computation.40 | convolution fusion | flops 6444023808 | bytes 18352128 | tf_op jit(solution)/shard_map/dot_general | solution.py:68
  194.3 3.2 concatenate.18
  197.5 2.9 copy.84
  201.1 1.4 fusion.24
  202.5 1.7 fusion.64
  205.2 2.3 copy.87
  207.5 3.2 reshape.259
  210.7 8.9 %convolution_convert_fusion = bf16[1024,4096]{1,0:T(8,128)(2,1)} fusion(bf16[1024,512]{1,0:T(8,128)(2,1)S(1)} %reshape.259, bf16[512,4096]{1,0:T(8,128)(2,1)} %param.29), kind=kOutput, calls=%fused_computation.25 | convolution fusion | flops 4299161600 | bytes 13631488 | tf_op jit(solution)/shard_map/dot_general | solution.py:206
  220.0 1.3 constant_dynamic-slice_fusion.1
  221.4 1.5 pad_maximum_fusion.1
  222.9 77.8 %reduce-scatter.6.cloned.1.call-done = bf16[256,4096]{1,0:T(8,128)(2,1)} async-done(((bf16[1024,4096]{1,0:T(8,128)(2,1)}), bf16[256,4096]{1,0:T(8,128)(2,1)}) %reduce-scatter.6.cloned.1.call-update) | async-done | bytes 2097168 | tf_op jit(solution)/shard_map/reduce_scatter | solution.py:205
  300.7 4.3 fusion.13
  305.0 9.5 %copy.97 = bf16[512,8,2,512]{3,1,2,0:T(8,128)(2,1)} copy(bf16[512,8,2,512]{3,2,1,0:T(2,128)(2,1)} %bitcast.119) | data formatting | bytes 16777216
  314.5 73.3 %all-gather.11.cloned.1.call-done = bf16[1024,4096]{1,0:T(8,128)(2,1)} async-done(((bf16[256,4096]{1,0:T(8,128)(2,1)}), bf16[1024,4096]{1,0:T(8,128)(2,1)}) %all-gather.11.cloned.1.call-update) | async-done | bytes 8388624 | tf_op jit(solution)/shard_map/all_gather | solution.py:217
  387.8 5.2 %fusion.6 = f32[1024]{0:T(1024)S(1)} fusion(bf16[1024,4096]{1,0:T(8,128)(2,1)} %all-gather.11.cloned.1.call-done), kind=kLoop, calls=%fused_computation.16 | loop fusion | flops 12581888 | bytes 8392704 | tf_op jit(solution)/shard_map/reduce_sum | solution.py:52
  393.6 11.2 %multiply_convert_fusion = bf16[1024,1024]{1,0:T(8,128)(2,1)S(1)} fusion(bf16[4096,1024]{1,0:T(8,128)(2,1)} %bitcast.120, bf16[1024,4096]{1,0:T(8,128)(2,1)S(1)} %copy-done.2, f32[4096]{0:T(1024)S(1)} %copy-done.9, f32[1024]{0:T(1024)S(1)} %add_rsqrt_fusion.1), kind=kOutput, calls=%fused_computation.33 | convolution fusion | flops 8604614656 | bytes 18894848 | tf_op jit(solution)/shard_map/dot_general | solution.py:54
  404.8 1.1 fusion.63
  406.0 17.6 %all_to_all.45 = bf16[4,256,512]{2,1,0:T(8,128)(2,1)S(1)} all-to-all(bf16[4,256,512]{2,1,0:T(8,128)(2,1)S(1)} %bitcast.128), channel_id=1, replica_groups=mesh['cache'=32,'psg'=4] {'psg'}, dimensions={0} | all-to-all | bytes 2097152 | tf_op jit(solution)/shard_map/all_to_all | solution.py:226
  423.5 3.5 all-to-all-start.3
  427.5 3.0 fusion.40
  430.4 13.7 %all_gather.49 = bf16[32,2048]{1,0:T(8,128)(2,1)S(1)} all-gather(bf16[32,512]{1,0:T(8,128)(2,1)S(1)} %fusion.40), channel_id=1, replica_groups=mesh['cache'=32,'psg'=4] {'psg'}, dimensions={1}, use_global_device_ids=true | all-gather | bytes 163840 | tf_op jit(solution)/shard_map/all_gather | solution.py:229
  444.4 1.3 copy.88
  446.3 1.6 fusion.65
  447.9 1.3 convolution_bitcast_fusion
  450.0 9.0 %all-gather.1 = f32[128,32]{1,0:T(8,128)S(1)} all-gather(f32[32,32]{1,0:T(8,128)S(1)} %copy.91), channel_id=3, replica_groups=mesh['cache'=32,'psg'=4] {'psg'}, dimensions={0}, use_global_device_ids=true | all-gather | bytes 20480 | tf_op jit(solution)/shard_map/all_gather | solution.py:14
  459.0 9.4 %all-gather = f32[128,32]{1,0:T(8,128)S(1)} all-gather(f32[32,32]{1,0:T(8,128)S(1)} %copy.90), channel_id=2, replica_groups=mesh['cache'=32,'psg'=4] {'psg'}, dimensions={0}, use_global_device_ids=true | all-gather | bytes 20480 | tf_op jit(solution)/shard_map/all_gather | solution.py:14
  468.4 16.0 %all-gather.13.cloned.1.call-done = f32[128,32,64]{2,0,1:T(8,128)} async-done(((f32[32,32,64]{2,0,1:T(8,128)}), f32[128,32,64]{2,0,1:T(8,128)}) %all-gather.13.cloned.1.call-update) | async-done | bytes 1048592 | tf_op jit(solution)/shard_map/all_gather | solution.py:14
  485.8 5.2 while.19
  485.8 1.1 constant_dynamic-slice_fusion.3
  487.5 1.1 constant_dynamic-slice_fusion.3
  491.4 3.8 convolution_convert_fusion.1
  495.3 18.6 %reduce-scatter.8.cloned.1.call-done = bf16[32,1024]{1,0:T(8,128)(2,1)} async-done(((bf16[32,4096]{1,0:T(8,128)(2,1)}), bf16[32,1024]{1,0:T(8,128)(2,1)}) %reduce-scatter.8.cloned.1.call-update) | async-done | bytes 65552 | tf_op jit(solution)/shard_map/reduce_scatter | solution.py:258
  (98 shorter events, 13.3 us)
Async XLA Ops:
  8.0 43.6 %copy-start = (bf16[1004,1024]{1,0:T(8,128)(2,1)S(1)}, bf16[1004,1024]{1,0:T(8,128)(2,1)}, u32[]{:S(2)}) copy-start(bf16[1004,1024]{1,0:T(8,128)(2,1)} %param.25) | copy-start | bytes 6168580
  8.0 139.0 %reduce-scatter.4.cloned.1.call-start = ((), (), s32[]{:S(2)}) async-start(), calls=%async_computation.8 | async-start | bytes 3244032 | tf_op jit(solution)/shard_map/reduce_scatter | solution.py:134
  51.6 4.9 copy-start.12
  51.6 6.2 %copy-start.10 = (s32[1,8]{1,0:T(1,128)S(1)}, s32[1,8]{1,0:T(1,128)}, u32[]{:S(2)}) copy-start(s32[1,8]{1,0:T(1,128)} %param.22) | copy-start | bytes 100
  51.6 6.3 %copy-start.11 = (s32[1,8,1]{1,2,0:T(1,128)S(1)}, s32[1,8,1]{1,2,0:T(1,128)}, u32[]{:S(2)}) copy-start(s32[1,8,1]{1,2,0:T(1,128)} %param.21) | copy-start | bytes 100
  56.4 25.3 %copy-start.3 = (bf16[32,16,1024]{2,1,0:T(8,128)(2,1)S(1)}, bf16[32,16,1024]{2,1,0:T(8,128)(2,1)}, u32[]{:S(2)}) copy-start(bf16[32,16,1024]{2,1,0:T(8,128)(2,1)} %param.24) | copy-start | bytes 3145732
  87.0 39.1 %all-to-all-start.1 = ((bf16[32,2,16,1024]{3,2,1,0:T(8,128)(2,1)}), bf16[32,2,16,1024]{3,2,1,0:T(8,128)(2,1)}, u32[]{:S(2)}, u32[]{:S(2)}) async-start(bf16[32,2,16,1024]{3,2,1,0:T(8,128)(2,1)} %broadcast_select_fusion), calls=%async_computation.1 | async-start | bytes 4194304 | tf_op jit(solution)/shard_map/all_to_all | solution.py:164
  92.0 85.4 %all-gather.9.cloned.1.call-start = ((), (), s32[]{:S(2)}) async-start(), calls=%async_computation.7 | async-start | bytes 5242880 | tf_op jit(solution)/shard_map/all_gather | solution.py:174
  129.5 17.2 %copy-start.4 = (f32[32,1024]{1,0:T(8,128)S(1)}, f32[32,1024]{1,0:T(8,128)}, u32[]{:S(2)}) copy-start(f32[32,1024]{1,0:T(8,128)} %constant.125.clone) | copy-start | bytes 393220
  129.5 17.2 %copy-start.7 = (f32[8,32]{1,0:T(8,128)S(1)}, f32[8,32]{1,0:T(8,128)}, u32[]{:S(2)}) copy-start(f32[8,32]{1,0:T(8,128)} %param.28) | copy-start | bytes 3076
  129.5 30.6 %copy-start.5 = (f32[4096]{0:T(1024)S(1)}, f32[4096]{0:T(1024)}, u32[]{:S(2)}) copy-start(f32[4096]{0:T(1024)} %param.26) | copy-start | bytes 49156
  129.5 171.2 %reduce-scatter.6.cloned.1.call-start = ((), (), s32[]{:S(2)}) async-start(), calls=%async_computation.9 | async-start | bytes 10485760 | tf_op jit(solution)/shard_map/reduce_scatter | solution.py:205
  219.7 168.2 %all-gather.11.cloned.1.call-start = ((), (), s32[]{:S(2)}) async-start(), calls=%async_computation.10 | async-start | bytes 10485760 | tf_op jit(solution)/shard_map/all_gather | solution.py:217
  305.0 88.0 %copy-start.9 = (f32[4096]{0:T(1024)S(1)}, f32[4096]{0:T(1024)}, u32[]{:S(2)}) copy-start(f32[4096]{0:T(1024)} %param.30) | copy-start | bytes 49156
  387.8 5.8 %copy-start.2 = (bf16[1024,4096]{1,0:T(8,128)(2,1)S(1)}, bf16[1024,4096]{1,0:T(8,128)(2,1)}, u32[]{:S(2)}) copy-start(bf16[1024,4096]{1,0:T(8,128)(2,1)} %all-gather.11.cloned.1.call-done) | copy-start | bytes 25165828
  404.8 22.3 %copy-start.8 = (f32[1,8]{1,0:T(1,128)S(1)}, f32[1,8]{1,0:T(1,128)}, u32[]{:S(2)}) copy-start(f32[1,8]{1,0:T(1,128)} %param.23) | copy-start | bytes 100
  404.8 22.6 %copy-start.6 = (f32[4096]{0:T(1024)S(1)}, f32[4096]{0:T(1024)}, u32[]{:S(2)}) copy-start(f32[4096]{0:T(1024)} %param.32) | copy-start | bytes 49156
  423.5 22.2 %all-to-all-start.3 = ((bf16[4,256,512]{2,1,0:T(8,128)(2,1)}), bf16[4,256,512]{2,1,0:T(8,128)(2,1)S(1)}, u32[]{:S(2)}, u32[]{:S(2)}) async-start(bf16[4,256,512]{2,1,0:T(8,128)(2,1)} %bitcast.127), calls=%async_computation.5 | async-start | bytes 2097152 | tf_op jit(solution)/shard_map/all_to_all | solution.py:227
  427.1 57.3 %all-gather.13.cloned.1.call-start = ((), (), s32[]{:S(2)}) async-start(), calls=%async_computation.12 | async-start | bytes 2621440 | tf_op jit(solution)/shard_map/all_gather | solution.py:14
  449.2 64.7 %reduce-scatter.8.cloned.1.call-start = ((), (), s32[]{:S(2)}) async-start(), calls=%async_computation.11 | async-start | bytes 327680 | tf_op jit(solution)/shard_map/reduce_scatter | solution.py:258
  491.0 23.0 %copy-start.1 = (bf16[1004,1024]{1,0:T(8,128)(2,1)S(1)}, bf16[1004,1024]{1,0:T(8,128)(2,1)}, u32[]{:S(2)}) copy-start(bf16[1004,1024]{1,0:T(8,128)(2,1)} %param.25) | copy-start | bytes 6168580
Sparse Core Ops, SparseCore 0:
  56.6 87.4 reduce-scatter.3
Sparse Core Ops, SparseCore 1:
  129.6 47.8 all-gather.8
  219.7 80.9 reduce-scatter.5
  305.1 82.7 all-gather.10
  449.3 35.0 all-gather.12
  495.4 18.5 reduce-scatter.7
where the time goes:
time: 525 us; the launch traced here: 522 us
  waiting for transfers between devices  229 us (44%)
  blocking collectives  128 us (24%)
  matrix products  56.4 us (11%)
  local copies, waits for them, and re-layouts  55.6 us (11%)
  other arithmetic  26.7 us (5%)
  between operations  16.8 us (3%)
  starting transfers between devices  9.25 us (2%)
    reduce_scatter x1, waiting for transfers between devices, shards(): lax.psum_scatter(jnp.dot(context, live_out, preferred_element_type=jnp.fl...  77.8 us
    all_gather x1, waiting for transfers between devices, shards(): lax.all_gather(encoded_rows, 'psg', axis=0, tiled=True)  73.3 us
    all_to_all x1, waiting for transfers between devices, shards(): lax.all_to_all(looked_up, 'cache', split_axis=0, concat_axis=0, tiled=True)  34 us
    unnamed x33, local copies, waits for them, and re-layouts  27.9 us
    all_gather x1, blocking collectives, shards(): lax.all_gather(question_ids, 'cache', axis=0, tiled=True)  23.2 us
    dot_general x3, matrix products, norm_project(): projected = jnp.dot(scaled, weights, preferred_element_type=jnp.float32)  22.2 us
    all_gather x1, blocking collectives, shards(): lax.all_gather(answer_ids, 'cache', axis=0, tiled=True)  20.2 us
    reduce_scatter x1, waiting for transfers between devices, shards(): lax.psum_scatter(jnp.dot(cross_context, cross_out, preferred_element_type...  18.6 us
  transfers between devices with their start and end apart: 8, of which 6 were waited for; matrix products, arithmetic and copies ran while one was open for 11% of the time, Pallas kernels for 0%

commit v1 on v0

v1 whole, which is shorter than its diff:
```python
import jax
import jax.numpy as jnp
import numpy as np
from jax import lax
from jax.sharding import PartitionSpec as P

HEAD = 64
EPSILON = 1e-06
F32 = jnp.float32
BF16 = jnp.bfloat16


def bucket_table(length, bucket_count):
    positions = np.arange(length)
    relative = positions[None, :] - positions[:, None]
    halfway = bucket_count // 2
    exact_span = halfway // 2
    upper_side = (relative > 0).astype(np.int64) * halfway
    distance = np.abs(relative)
    log_bucket = exact_span + (
        np.log(np.maximum(distance, 1) / exact_span)
        / np.log(128.0 / exact_span)
        * (halfway - exact_span)
    ).astype(np.int64)
    log_bucket = np.minimum(log_bucket, halfway - 1)
    return upper_side + np.where(distance < exact_span, distance, log_bucket)


def position_bias(bias_table, length):
    bucket_count = bias_table.shape[1]
    buckets = bucket_table(length, bucket_count).reshape(-1)
    onehot = (buckets[None, :] == np.arange(bucket_count)[:, None]).astype(np.float32)
    spread = jnp.dot(
        bias_table, jnp.asarray(onehot, dtype=bias_table.dtype), precision=lax.Precision.HIGHEST
    )
    return spread.reshape(bias_table.shape[0], length, length)


def norm_project(rows_in, gain_vector, weights):
    wide = rows_in.astype(F32)
    inverse = lax.rsqrt(jnp.mean(wide * wide, axis=-1, keepdims=True) + EPSILON)
    scaled = (wide * gain_vector).astype(BF16)
    projected = jnp.dot(scaled, weights, preferred_element_type=F32)
    return (projected * inverse).astype(BF16)


def softmax_rows(scores):
    maximum = jnp.max(scores, axis=-1, keepdims=True)
    exponents = jnp.exp(scores - maximum)
    return (exponents / jnp.sum(exponents, axis=-1, keepdims=True)).astype(BF16)


def dot32(a, b, dims):
    return lax.dot_general(a, b, (dims, ((), ())), preferred_element_type=F32)


def shards(
    question_ids, answer_ids, owner, slot, passage_score, memory, embedding, live_gain, live_qkv,
    rel_bias, live_out, enc_gain, cross_kv, dec_gain, cross_query, cross_out,
):
    n_cache = lax.axis_size("cache")
    n_psg = lax.axis_size("psg")
    me_c = lax.axis_index("cache")
    me_z = lax.axis_index("psg")
    width = live_gain.shape[0]
    plen = memory.shape[1]
    qlen = question_ids.shape[1]
    alen = answer_ids.shape[1]
    own_count = owner.shape[1]
    total = own_count * n_psg
    seq = plen + qlen
    heads = rel_bias.shape[0]
    cols = live_out.shape[0]
    scale = HEAD ** (-0.5)

    piece_rows = cols // n_cache
    piece = lax.dynamic_slice_in_dim(live_out, me_c * piece_rows, piece_rows, 0)
    pieces = lax.all_gather(piece, "psg", axis=0, tiled=False)
    out_full = [lax.all_gather(pieces[z], "cache", axis=0, tiled=True) for z in range(n_psg)]

    ints = jnp.concatenate(
        [question_ids[0], answer_ids[0], owner[0, :, 0], slot[0]], axis=0
    ).reshape(1, 1, -1)
    every = lax.all_gather(ints, ("cache", "psg"), axis=0, tiled=True).reshape(n_cache, n_psg, -1)
    tokens = every[:, 0, : qlen + alen]
    owners = every[:, :, qlen + alen : qlen + alen + own_count].reshape(n_cache, total)
    slots = every[:, :, qlen + alen + own_count :].reshape(n_cache, total)
    order = jnp.arange(total)
    earlier = (owners[:, :, None] == owners[:, None, :]) & (order[None, :] < order[:, None])[None]
    rank = jnp.sum(earlier, axis=2)
    mine = owners == me_c
    asked = jnp.sum(
        jnp.where(mine[:, None, :] & (rank[:, None, :] == jnp.arange(2)[None, :, None]),
                  slots[:, None, :], 0),
        axis=2,
    )
    place = lax.dynamic_index_in_dim(owners * 2 + rank, me_c, 0, False)
    looked_up = jnp.take(memory, asked.reshape(-1), axis=0).reshape((n_cache, 2) + memory.shape[1:])
    fetched = lax.all_to_all(looked_up, "cache", split_axis=0, concat_axis=0, tiled=True)
    slices = jnp.take(fetched.reshape((-1,) + memory.shape[1:]), place, axis=0)
    x_mem = lax.all_gather(slices, "psg", axis=2, tiled=True).reshape(total * plen, width)

    vocab = embedding.shape[0]
    onehot = (
        (tokens - me_c * vocab)[:, :, None] == jnp.arange(vocab, dtype=jnp.int32)
    ).astype(BF16)
    token_slice = lax.psum_scatter(
        jnp.einsum("qtv,vf->qtf", onehot, embedding, preferred_element_type=F32).astype(BF16),
        "cache", scatter_dimension=0, tiled=True,
    )
    token_full = lax.all_gather(token_slice, "psg", axis=2, tiled=True)[0]
    x_q = token_full[:qlen]
    answer = token_full[qlen:]
    score_all = lax.all_gather(passage_score[0], "psg", axis=0, tiled=True)

    q_dec = norm_project(answer, dec_gain, cross_query).reshape(alen, heads, HEAD)
    w_key = cross_kv[:, 0].reshape(width, heads, HEAD)
    w_val = cross_kv[:, 1].reshape(width, heads, HEAD)
    qg = (
        jnp.einsum("thd,fhd->htf", q_dec, w_key, preferred_element_type=F32) * enc_gain
    ).astype(BF16).reshape(heads * alen, width)
    ql = [dot32(qg, o, ((1,), (1,))).astype(BF16) for o in out_full]

    w_qkv = live_qkv.reshape(width, 3 * cols)
    mem_proj = norm_project(x_mem, live_gain, w_qkv).reshape(total, plen, 3 * cols)
    q_proj = norm_project(x_q, live_gain, w_qkv)
    proj = jnp.concatenate(
        [mem_proj, jnp.broadcast_to(q_proj[None], (total, qlen, 3 * cols))], axis=1
    ).reshape(total, seq, 3, heads, HEAD)
    scores = jnp.einsum(
        "pqhd,pkhd->phqk", proj[:, :, 0], proj[:, :, 1], preferred_element_type=F32
    ) * scale + position_bias(rel_bias, seq)[None]
    ctx = (
        jnp.einsum("phqk,pkhd->pqhd", softmax_rows(scores), proj[:, :, 2],
                   preferred_element_type=F32)
        .astype(BF16).reshape(total * seq, cols)
    )
    ctx_all = lax.all_gather(ctx, "psg", axis=0, tiled=False)

    own_rows = own_count * seq
    own_ctx = lax.dynamic_slice_in_dim(ctx_all, me_z * own_rows, own_rows, 1)
    attended = sum(
        dot32(own_ctx[z], out_full[z], ((1,), (0,))).astype(BF16).astype(F32) for z in range(n_psg)
    )
    own_mem = lax.dynamic_slice_in_dim(x_mem, me_z * own_count * plen, own_count * plen, 0)
    own_input = jnp.concatenate(
        [own_mem.reshape(own_count, plen, width),
         jnp.broadcast_to(x_q[None], (own_count, qlen, width))], axis=1,
    ).reshape(own_rows, width)
    encoded = (own_input.astype(F32) + attended).astype(BF16)
    enc32 = encoded.astype(F32)
    inv_own = lax.rsqrt(jnp.mean(enc32 * enc32, axis=-1) + EPSILON)
    inv = lax.all_gather(inv_own, "psg", axis=0, tiled=True)

    s_mem = dot32(qg, x_mem, ((1,), (1,))).reshape(-1, total, plen)
    s_q = jnp.broadcast_to(dot32(qg, x_q, ((1,), (1,)))[:, None], (heads * alen, total, qlen))
    s = jnp.concatenate([s_mem, s_q], axis=2).reshape(heads * alen, total * seq)
    for z in range(n_psg):
        s = s + dot32(ql[z], ctx_all[z], ((1,), (1,)))
    s = s * (inv * scale)[None] + jnp.repeat(score_all, seq)[None]
    top = jnp.max(s, axis=-1, keepdims=True)
    e = jnp.exp(s - top)
    sums = jnp.sum(e, axis=-1, keepdims=True)
    w = (e * inv[None] / sums).astype(BF16)
    w3 = w.reshape(-1, total, seq)
    w_mem = w3[:, :, :plen].reshape(-1, total * plen)
    w_q = jnp.sum(w3[:, :, plen:].astype(F32), axis=1).astype(BF16)
    zed = dot32(w_mem, x_mem, ((1,), (0,))) + dot32(w_q, x_q, ((1,), (0,)))
    for z in range(n_psg):
        part = dot32(w, ctx_all[z], ((1,), (0,))).astype(BF16)
        zed = zed + dot32(part, out_full[z], ((1,), (0,)))
    zed = (zed * enc_gain).astype(BF16).reshape(heads, alen, width)
    context = jnp.einsum("htf,fhd->thd", zed, w_val, preferred_element_type=F32).astype(BF16)
    decoded = lax.psum_scatter(
        dot32(context.reshape(alen, -1), cross_out, ((1,), (0,))).astype(BF16),
        "psg", scatter_dimension=1, tiled=True,
    )
    return encoded.reshape(1, own_count, seq, width), decoded[None]


def solution(mesh):
    return jax.shard_map(
        shards,
        mesh=mesh,
        in_specs=(
            P("cache", None), P("cache", None), P("cache", "psg", None), P("cache", "psg"),
            P("cache", "psg"), P("cache", None, "psg"), P("cache", "psg"), P(),
            P(None, None, "psg"), P("psg", None), P("psg", None), P(), P(None, None, "psg"), P(),
            P(None, "psg"), P("psg", None),
        ),
        out_specs=(P("cache", "psg", None, None), P("cache", None, "psg")),
        check_vma=False,
    )
```

time: 525 us -> 532 us (1.013); the launches traced: 522 us -> 523 us
  waiting for transfers between devices: 229 us -> 144 us
  matrix products: 56.4 us -> 123 us
  local copies, waits for them, and re-layouts: 55.6 us -> 106 us
  blocking collectives: 128 us -> 111 us
  other arithmetic: 26.7 us -> 15.5 us
    reduce_scatter x2 -> x1, waiting for transfers between devices: 96.4 us -> 17.3 us  [shards(): lax.psum_scatter(dot32(context.reshape(alen, -1), cross_out, ((1,), (0,))...]
    unnamed x1 -> x2, blocking collectives: 7.71 us -> 78.5 us
    dot_general x11 -> x25, matrix products: 56.2 us -> 123 us  [the longest x17 85.8 us: dot32(): return lax.dot_general(a, b, (dims, ((), ())), preferred_element_type=F32)]
    all_gather x6 -> x3, blocking collectives: 88.4 us -> 32.8 us  [the longest x1 13.1 us: shards(): token_full = lax.all_gather(token_slice, 'psg', axis=2, tiled=True)[0]]
    slice x1 -> x7, local copies, waits for them, and re-layouts: 1.13 us -> 55.3 us  [the longest x2 35.8 us: shards(): w_val = cross_kv[:, 1].reshape(width, heads, HEAD)]
    all_to_all x2 -> x0, blocking collectives: 31.8 us -> none  [the longest x1 17.6 us: shards(): lax.all_to_all(key_block, 'psg', split_axis=0, concat_axis=2, tiled=True)]
    unnamed x33 -> x31, local copies, waits for them, and re-layouts: 27.9 us -> 17.8 us
    all_to_all x1, waiting for transfers between devices: 34 us -> 27.9 us  [shards(): lax.all_to_all(looked_up, 'cache', split_axis=0, concat_axis=0, tiled=True)]
  transfers between devices with their start and end apart: 8 -> 9, of which waited for: 6 -> 5; matrix products, arithmetic and copies ran while one was open for 11% -> 32% of each run, Pallas kernels for 0% -> 0%
where the time goes in v1:
time: 532 us; the launch traced here: 523 us
  waiting for transfers between devices  144 us (27%)
  matrix products  123 us (23%)
  blocking collectives  111 us (21%)
  local copies, waits for them, and re-layouts  106 us (20%)
  between operations  16.9 us (3%)
  other arithmetic  15.5 us (3%)
  starting transfers between devices  5.5 us (1%)
    all_gather x4, waiting for transfers between devices, shards(): lax.all_gather(pieces[z], 'cache', axis=0, tiled=True)  97 us
    dot_general x17, matrix products, dot32(): return lax.dot_general(a, b, (dims, ((), ())), preferred_element_type=F32)  85.8 us
    unnamed x2, blocking collectives  78.5 us
    slice x2, local copies, waits for them, and re-layouts, shards(): w_val = cross_kv[:, 1].reshape(width, heads, HEAD)  35.8 us
    all_to_all x1, waiting for transfers between devices, shards(): lax.all_to_all(looked_up, 'cache', split_axis=0, concat_axis=0, tiled=True)  27.9 us
    dot_general x3, matrix products, norm_project(): projected = jnp.dot(scaled, weights, preferred_element_type=F32)  23 us
    slice x1, local copies, waits for them, and re-layouts, shards(): w_key = cross_kv[:, 0].reshape(width, heads, HEAD)  18.4 us
    unnamed x31, local copies, waits for them, and re-layouts  17.8 us
  transfers between devices with their start and end apart: 9, of which 5 were waited for; matrix products, arithmetic and copies ran while one was open for 32% of the time, Pallas kernels for 0%

profile of v1, /device:TPU:1, one launch (start us, length us, event | category | flops | bytes accessed | tf_op | source)
XLA Modules:
  0.0 523.1 jit_solution(1231734913170525342)
XLA Ops:
  9.1 68.8 %all-reduce = s32[8192]{0:T(1024)S(1)} all-reduce(s32[8192]{0:T(1024)S(1)} %add_dynamic-update-slice_fusion), channel_id=2, replica_groups=mesh['cache'=32,'psg'=4] {'cache','psg'}, use_global_device_ids=true, to_apply=%add | all-reduce | flops 8192 | bytes 65536
  78.0 4.8 fusion.19
  84.7 2.0 gather_fusion
  86.7 3.2 broadcast_select_fusion
  89.9 5.2 all-to-all-start
  95.2 27.9 %all-to-all-done = bf16[32,2,16,1024]{3,2,1,0:T(8,128)(2,1)} async-done(((bf16[32,2,16,1024]{3,2,1,0:T(8,128)(2,1)}), bf16[32,2,16,1024]{3,2,1,0:T(8,128)(2,1)}, u32[]{:S(2)}, u32[]{:S(2)}) %all-to-all-start) | async-done | bytes 2097184 | tf_op jit(solution)/shard_map/all_to_all | solution.py:99
  123.1 2.2 gather_fusion.1
  125.3 2.2 copy_select_fusion
  128.5 11.7 %all-gather.1 = bf16[64,4096]{1,0:T(8,128)(2,1)S(1)} all-gather(bf16[16,4096]{1,0:T(8,128)(2,1)S(1)} %constant_dynamic-slice_fusion.1), channel_id=3, replica_groups=mesh['cache'=32,'psg'=4] {'psg'}, dimensions={0}, use_global_device_ids=true | all-gather | bytes 655360 | tf_op jit(solution)/shard_map/all_gather | solution.py:78
  141.1 17.0 %copy.111 = bf16[4096,3,512]{0,2,1:T(8,128)(2,1)} copy(bf16[4096,3,512]{2,0,1:T(8,128)(2,1)} %param.25) | data formatting | bytes 25165824 | tf_op args[8]
  158.6 13.1 %all_gather.38 = bf16[1,48,4096]{2,1,0:T(8,128)(2,1)S(1)} all-gather(bf16[1,48,1024]{2,1,0:T(8,128)(2,1)} %reduce-scatter.3.cloned.1.call-done), channel_id=1, replica_groups=mesh['cache'=32,'psg'=4] {'psg'}, dimensions={2}, use_global_device_ids=true | all-gather | bytes 491520 | tf_op jit(solution)/shard_map/all_gather | solution.py:111
  171.8 7.9 %fusion.20 = bf16[16,1536]{1,0:T(8,128)(2,1)S(1)} fusion(bf16[4096,1536]{0,1:T(8,128)(2,1)} %bitcast.152, f32[4096]{0:T(1024)S(1)} %copy-done.7, bf16[1,48,4096]{2,1,0:T(8,128)(2,1)S(1)} %all_gather.38, f32[16]{0:T(128)S(1)} %add_rsqrt_fusion.3), kind=kOutput, calls=%fused_computation.47 | convolution fusion | flops 201572352 | bytes 12780032 | tf_op jit(solution)/shard_map/dot_general | solution.py:43
  179.9 3.8 fusion.2
  183.8 4.2 copy.110
  188.2 12.1 %fusion.18 = bf16[512,1536]{1,0:T(8,128)(2,1)} fusion(bf16[512,4096]{1,0:T(8,128)(2,1)} %bitcast.166, bf16[4096,1536]{0,1:T(8,128)(2,1)} %bitcast.153, f32[512]{0:T(512)S(1)} %rsqrt.31), kind=kOutput, calls=%fused_computation.44 | convolution fusion | flops 6444023808 | bytes 18352128 | tf_op jit(solution)/shard_map/dot_general | solution.py:43
  200.2 5.1 concatenate.17
  205.3 2.9 copy.114
  210.3 1.7 fusion.70
  213.1 2.3 copy.117
  215.4 4.1 all_gather_reshape.3
  221.7 17.4 %fusion.67 = (bf16[4096,1,512]{2,1,0:T(2,128)(2,1)}, bf16[4096,1,512]{2,1,0:T(2,128)(2,1)}) fusion(bf16[4096,2,512]{2,1,0:T(2,128)(2,1)} %param.29), kind=kLoop, calls=%fused_computation.149 | loop fusion | bytes 16777216 | tf_op jit(solution)/shard_map/slice | solution.py:118
  239.2 18.4 %copy.118 = bf16[4096,1,512]{0,2,1:T(8,128)(2,1)} copy(bf16[4096,1,512]{2,1,0:T(2,128)(2,1)} %get-tuple-element.5) | data formatting | bytes 8388608 | tf_op jit(solution)/shard_map/slice | solution.py:117
  259.0 9.7 %all-reduce.1 = f32[32]{0:T(128)S(1)} all-reduce(f32[32]{0:T(128)S(1)} %bitcast_dynamic-update-slice_fusion), channel_id=8, replica_groups=mesh['cache'=32,'psg'=4] {'psg'}, use_global_device_ids=true, to_apply=%add.1 | all-reduce | flops 32 | bytes 256
  268.8 18.4 %copy.124 = bf16[4096,1,512]{0,2,1:T(8,128)(2,1)} copy(bf16[4096,1,512]{2,1,0:T(2,128)(2,1)} %get-tuple-element.4) | data formatting | bytes 8388608 | tf_op jit(solution)/shard_map/slice | solution.py:118
  287.3 3.0 fusion.41
  290.5 3.1 fusion.6
  297.6 4.5 copy.109
  303.9 5.5 %fusion.15 = f32[256,4096]{1,0:T(8,128)} fusion(bf16[512,4096]{1,0:T(8,128)(2,1)} %all-gather.23.cloned.1.call-done, bf16[4,1024,512]{2,1,0:T(8,128)(2,1)} %all-gather.21.cloned.1.call-done, s32[]{:T(128)S(6)} %select_n.68), kind=kOutput, calls=%fused_computation.35 | convolution fusion | flops 1075838976 | bytes 8650756 | tf_op jit(solution)/shard_map/dot_general | solution.py:54
  309.3 14.3 %all-gather.25.cloned.1.call-done = bf16[512,4096]{1,0:T(8,128)(2,1)} async-done(((bf16[16,4096]{1,0:T(8,128)(2,1)}), bf16[512,4096]{1,0:T(8,128)(2,1)}) %all-gather.25.cloned.1.call-update) | async-done | bytes 4194320 | tf_op jit(solution)/shard_map/all_gather | solution.py:79
  323.6 6.8 %fusion.14 = f32[256,4096]{1,0:T(8,128)} fusion(f32[256,4096]{1,0:T(8,128)} %fusion.15, bf16[512,4096]{1,0:T(8,128)(2,1)} %all-gather.25.cloned.1.call-done, bf16[4,1024,512]{2,1,0:T(8,128)(2,1)} %all-gather.21.cloned.1.call-done, s32[]{:T(128)S(6)} %add.205, s32[]{:T(128)S(6)} %select_n.68), kind=kOutput, calls=%fused_computation.33 | convolution fusion | flops 1076887552 | bytes 12845064 | tf_op jit(solution)/shard_map/dot_general | solution.py:54
  330.4 41.4 %all-gather.27.cloned.1.call-done = bf16[512,4096]{1,0:T(8,128)(2,1)} async-done(((bf16[16,4096]{1,0:T(8,128)(2,1)}), bf16[512,4096]{1,0:T(8,128)(2,1)}) %all-gather.27.cloned.1.call-update) | async-done | bytes 4194320 | tf_op jit(solution)/shard_map/all_gather | solution.py:79
  371.7 6.8 %fusion.12 = f32[256,4096]{1,0:T(8,128)} fusion(f32[256,4096]{1,0:T(8,128)} %fusion.14, bf16[512,4096]{1,0:T(8,128)(2,1)} %all-gather.27.cloned.1.call-done, bf16[4,1024,512]{2,1,0:T(8,128)(2,1)} %all-gather.21.cloned.1.call-done, s32[]{:T(128)S(6)} %add.206, s32[]{:T(128)S(6)} %select_n.68), kind=kOutput, calls=%fused_computation.30 | convolution fusion | flops 1076887552 | bytes 12845064 | tf_op jit(solution)/shard_map/dot_general | solution.py:54
  378.5 41.4 %all-gather.29.cloned.1.call-done = bf16[512,4096]{1,0:T(8,128)(2,1)} async-done(((bf16[16,4096]{1,0:T(8,128)(2,1)}), bf16[512,4096]{1,0:T(8,128)(2,1)}) %all-gather.29.cloned.1.call-update) | async-done | bytes 4194320 | tf_op jit(solution)/shard_map/all_gather | solution.py:79
  419.9 7.0 %multiply_reduce_fusion = (f32[256]{0:T(256)S(1)}, bf16[256,4096]{1,0:T(8,128)(2,1)}) fusion(f32[256,4096]{1,0:T(8,128)} %fusion.12, bf16[512,4096]{1,0:T(8,128)(2,1)} %all-gather.29.cloned.1.call-done, bf16[4,1024,512]{2,1,0:T(8,128)(2,1)} %all-gather.21.cloned.1.call-done, s32[]{:T(128)S(6)} %add.207, s32[]{:T(128)S(6)} %select_n.68, ...), kind=kOutput, calls=%fused_computation.37 | convolution fusion | flops 1083178752 | bytes 12846088 | tf_op jit(solution)/shard_map/dot_general | solution.py:54
  426.8 8.1 %all-gather.11 = f32[4,1,256]{2,1,0:T(1,128)S(1)} all-gather(f32[1,1,256]{2,1,0:T(1,128)S(1)} %bitcast.176), channel_id=1, replica_groups=mesh['cache'=32,'psg'=4] {'psg'}, dimensions={0}, use_global_device_ids=true | all-gather | bytes 5120 | tf_op jit(solution)/shard_map/all_gather | solution.py:153
  434.9 4.7 convolution_add_fusion.8
  439.6 4.7 convolution_add_fusion.7
  444.4 4.7 convolution_add_fusion.6
  449.1 4.8 fusion.71
  454.8 3.5 convolution_bitcast_fusion
  458.4 2.7 convolution_add_fusion.4
  461.0 7.3 %convolution_add_fusion.3 = f32[256,4096]{1,0:T(8,128)} fusion(f32[256,4096]{1,0:T(8,128)} %convolution_add_fusion.4, bf16[512,4096]{1,0:T(8,128)(2,1)} %all-gather.23.cloned.1.call-done, bf16[256,1024]{1,0:T(8,128)(2,1)S(1)} %divide_convert_fusion.4, bf16[4,1024,512]{2,1,0:T(8,128)(2,1)} %all-gather.21.cloned.1.call-done), kind=kOutput, calls=%fused_computation.17 | convolution fusion | flops 1343356928 | bytes 14155776 | tf_op jit(solution)/shard_map/dot_general | solution.py:54
  468.4 7.3 %convolution_add_fusion.2 = f32[256,4096]{1,0:T(8,128)} fusion(f32[256,4096]{1,0:T(8,128)} %convolution_add_fusion.3, bf16[512,4096]{1,0:T(8,128)(2,1)} %all-gather.25.cloned.1.call-done, bf16[256,1024]{1,0:T(8,128)(2,1)S(1)} %divide_convert_fusion.4, bf16[4,1024,512]{2,1,0:T(8,128)(2,1)} %all-gather.21.cloned.1.call-done), kind=kOutput, calls=%fused_computation.16 | convolution fusion | flops 1343356928 | bytes 14155776 | tf_op jit(solution)/shard_map/dot_general | solution.py:54
  475.7 7.6 %convolution_add_fusion.1 = f32[256,4096]{1,0:T(8,128)} fusion(f32[256,4096]{1,0:T(8,128)} %convolution_add_fusion.2, bf16[512,4096]{1,0:T(8,128)(2,1)} %all-gather.27.cloned.1.call-done, bf16[256,1024]{1,0:T(8,128)(2,1)S(1)} %divide_convert_fusion.4, bf16[4,1024,512]{2,1,0:T(8,128)(2,1)} %all-gather.21.cloned.1.call-done), kind=kOutput, calls=%fused_computation.15 | convolution fusion | flops 1343356928 | bytes 14155776 | tf_op jit(solution)/shard_map/dot_general | solution.py:54
  483.3 6.7 %fusion.5 = bf16[256,4096]{1,0:T(8,128)(2,1)} fusion(f32[256,4096]{1,0:T(8,128)} %convolution_add_fusion.1, bf16[512,4096]{1,0:T(8,128)(2,1)} %all-gather.29.cloned.1.call-done, f32[4096]{0:T(1024)S(1)} %copy-done.8, bf16[256,1024]{1,0:T(8,128)(2,1)S(1)} %divide_convert_fusion.4, bf16[4,1024,512]{2,1,0:T(8,128)(2,1)} %all-gather.21.cloned.1.call-done), kind=kOutput, calls=%fused_computation.21 | convolution fusion | flops 1345454080 | bytes 12075008 | tf_op jit(solution)/shard_map/dot_general | solution.py:54
  490.0 4.2 fusion.40
  494.3 3.7 convolution_convert_fusion.4
  498.1 17.3 %reduce-scatter.5.cloned.1.call-done = bf16[32,1024]{1,0:T(8,128)(2,1)} async-done(((bf16[32,4096]{1,0:T(8,128)(2,1)}), bf16[32,1024]{1,0:T(8,128)(2,1)}) %reduce-scatter.5.cloned.1.call-update) | async-done | bytes 65552 | tf_op jit(solution)/shard_map/reduce_scatter | solution.py:174
  (110 shorter events, 19.2 us)
Async XLA Ops:
  8.0 70.0 %copy-start = (bf16[1004,1024]{1,0:T(8,128)(2,1)S(1)}, bf16[1004,1024]{1,0:T(8,128)(2,1)}, u32[]{:S(2)}) copy-start(bf16[1004,1024]{1,0:T(8,128)(2,1)} %param.23) | copy-start | bytes 6168580
  8.0 150.5 %reduce-scatter.3.cloned.1.call-start = ((), (), s32[]{:S(2)}) async-start(), calls=%async_computation.4 | async-start | bytes 3244032 | tf_op jit(solution)/shard_map/reduce_scatter | solution.py:107
  82.9 1.8 copy-start.4
  89.9 33.2 %all-to-all-start = ((bf16[32,2,16,1024]{3,2,1,0:T(8,128)(2,1)}), bf16[32,2,16,1024]{3,2,1,0:T(8,128)(2,1)}, u32[]{:S(2)}, u32[]{:S(2)}) async-start(bf16[32,2,16,1024]{3,2,1,0:T(8,128)(2,1)} %broadcast_select_fusion), calls=%async_computation | async-start | bytes 4194304 | tf_op jit(solution)/shard_map/all_to_all | solution.py:99
  95.1 84.8 %all-gather.19.cloned.1.call-start = ((), (), s32[]{:S(2)}) async-start(), calls=%async_computation.3 | async-start | bytes 5242880 | tf_op jit(solution)/shard_map/all_gather | solution.py:101
  127.5 176.3 %all-gather.23.cloned.1.call-start = ((), (), s32[]{:S(2)}) async-start(), calls=%async_computation.7 | async-start | bytes 4325376 | tf_op jit(solution)/shard_map/all_gather | solution.py:79
  141.0 17.1 %copy-start.6 = (f32[32,1024]{1,0:T(8,128)S(1)}, f32[32,1024]{1,0:T(8,128)}, u32[]{:S(2)}) copy-start(f32[32,1024]{1,0:T(8,128)} %constant.84.clone) | copy-start | bytes 393220
  141.1 17.1 %copy-start.10 = (f32[8,32]{1,0:T(8,128)S(1)}, f32[8,32]{1,0:T(8,128)}, u32[]{:S(2)}) copy-start(f32[8,32]{1,0:T(8,128)} %param.26) | copy-start | bytes 3076
  141.1 30.7 %copy-start.7 = (f32[4096]{0:T(1024)S(1)}, f32[4096]{0:T(1024)}, u32[]{:S(2)}) copy-start(f32[4096]{0:T(1024)} %param.24) | copy-start | bytes 49156
  141.1 162.8 %all-gather.21.cloned.1.call-start = ((), (), s32[]{:S(2)}) async-start(), calls=%async_computation.5 | async-start | bytes 5242880 | tf_op jit(solution)/shard_map/all_gather | solution.py:138
  219.4 104.2 %all-gather.25.cloned.1.call-start = ((), (), s32[]{:S(2)}) async-start(), calls=%async_computation.8 | async-start | bytes 4325376 | tf_op jit(solution)/shard_map/all_gather | solution.py:79
  220.2 151.6 %all-gather.27.cloned.1.call-start = ((), (), s32[]{:S(2)}) async-start(), calls=%async_computation.9 | async-start | bytes 4325376 | tf_op jit(solution)/shard_map/all_gather | solution.py:79
  220.9 198.9 %all-gather.29.cloned.1.call-start = ((), (), s32[]{:S(2)}) async-start(), calls=%async_computation.10 | async-start | bytes 4325376 | tf_op jit(solution)/shard_map/all_gather | solution.py:79
  221.7 293.7 %reduce-scatter.5.cloned.1.call-start = ((), (), s32[]{:S(2)}) async-start(), calls=%async_computation.6 | async-start | bytes 327680 | tf_op jit(solution)/shard_map/reduce_scatter | solution.py:174
  239.1 18.5 %copy-start.12 = (u32[128]{0:T(128)S(1)}, u32[128]{0:T(128)}, u32[]{:S(2)}) copy-start(u32[128]{0:T(128)} %constant.97) | copy-start | bytes 1540
  239.1 19.7 %copy-start.11 = (f32[1,8]{1,0:T(1,128)S(1)}, f32[1,8]{1,0:T(1,128)}, u32[]{:S(2)}) copy-start(f32[1,8]{1,0:T(1,128)} %param.21) | copy-start | bytes 100
  268.8 18.5 %copy-start.9 = (f32[4096]{0:T(1024)S(1)}, f32[4096]{0:T(1024)}, u32[]{:S(2)}) copy-start(f32[4096]{0:T(1024)} %param.30) | copy-start | bytes 49156
  287.1 3.3 copy-start.8
  290.5 3.8 copy-start.2
  293.6 2.0 copy-start.3
  419.9 15.0 %copy-start.5 = (f32[256,1024]{1,0:T(8,128)S(1)}, f32[256,1024]{1,0:T(8,128)}, u32[]{:S(2)}) copy-start(f32[256,1024]{1,0:T(8,128)} %copy.121) | copy-start | bytes 3145732
  490.0 25.4 %copy-start.1 = (bf16[1004,1024]{1,0:T(8,128)(2,1)S(1)}, bf16[1004,1024]{1,0:T(8,128)(2,1)}, u32[]{:S(2)}) copy-start(bf16[1004,1024]{1,0:T(8,128)(2,1)} %param.23) | copy-start | bytes 6168580
Sparse Core Ops, SparseCore 0:
  83.0 75.3 reduce-scatter.2
Sparse Core Ops, SparseCore 1:
  127.6 49.4 all-gather.18
  179.2 45.9 all-gather.22
  226.8 47.4 all-gather.20
  276.8 46.7 all-gather.24
  326.2 45.5 all-gather.26
  374.3 45.5 all-gather.28
  498.2 17.2 reduce-scatter.4

commit v2 on v1

--- a/solution.py
+++ b/solution.py
@@ -1,7 +1,11 @@
+import functools
+
 import jax
 import jax.numpy as jnp
 import numpy as np
 from jax import lax
+from jax.experimental import pallas as pl
+from jax.experimental.pallas import tpu as pltpu
 from jax.sharding import PartitionSpec as P
 
 HEAD = 64
@@ -52,6 +56,503 @@
 
 def dot32(a, b, dims):
     return lax.dot_general(a, b, (dims, ((), ())), preferred_element_type=F32)
+
+
+MESH = pl.DeviceIdType.MESH
+VM = pl.BlockSpec(memory_space=pltpu.VMEM)
+SM = pl.BlockSpec(memory_space=pltpu.SMEM)
+ANY = pl.BlockSpec(memory_space=pl.ANY)
+
+
+def params(collective_id, mib):
+    return pltpu.CompilerParams(
+        collective_id=collective_id, has_side_effects=True, vmem_limit_bytes=mib << 20
+    )
+
+
+class Place:
+    def __init__(self):
+        self.c = lax.axis_index("cache")
+        self.z = lax.axis_index("psg")
+        self.core = lax.rem(self.c, 2)
+        self.x = lax.rem(lax.div(self.c, 2), 4)
+        self.y = lax.div(self.c, 8)
+
+    def cache(self, c):
+        return {"cache": c, "psg": self.z}
+
+    def chip(self, y, x):
+        return self.cache((y * 4 + x) * 2 + self.core)
+
+    def sibling(self):
+        return self.cache(self.c + 1 - 2 * self.core)
+
+    def up(self, z):
+        return {"cache": self.c, "psg": z}
+
+
+def turn(p, k):
+    return lax.rem(p + k + 4, 4)
+
+
+def greet_all(at):
+    barrier = pltpu.get_barrier_semaphore()
+
+    def greet(d, carry):
+        pl.semaphore_signal(
+            barrier, inc=1, device_id=at.cache(lax.rem(at.c + d, 32)), device_id_type=MESH
+        )
+        return carry
+
+    lax.fori_loop(1, 32, greet, 0)
+    for k in range(1, 4):
+        pl.semaphore_signal(barrier, inc=1, device_id=at.up(turn(at.z, k)), device_id_type=MESH)
+    pl.semaphore_wait(barrier, 34)
+
+
+class Mover:
+    def __init__(self, send, recv):
+        self.send, self.recv, self.count, self.started = send, recv, 0, []
+
+    def go(self, src, dst, device):
+        i = self.count
+        self.count += 1
+        copy = pltpu.make_async_remote_copy(
+            src_ref=src, dst_ref=dst, send_sem=self.send.at[i], recv_sem=self.recv.at[i],
+            device_id=device, device_id_type=MESH,
+        )
+        copy.start()
+        self.started.append(copy)
+        return copy
+
+    def finish_sends(self):
+        for copy in self.started:
+            copy.wait_send()
+
+
+class Ring:
+    def __init__(self, mover, pos, device, own, dst, units):
+        self.mover, self.pos, self.device, self.dst, self.units = mover, pos, device, dst, units
+        right, left = device(turn(pos, 1)), device(turn(pos, -1))
+        self.to_right, self.to_left = {}, {}
+        half = len(units) // 2
+        self.first, self.last = units[:half], units[half:]
+        for u, v in zip(units, self.last + self.first):
+            self.to_right[u] = mover.go(own(u), dst(pos, u, 1), right)
+            self.to_left[v] = mover.go(own(v), dst(pos, v, -1), left)
+
+    def onward(self):
+        right, left = self.device(turn(self.pos, 1)), self.device(turn(self.pos, -1))
+        self.far = []
+        for u, v in zip(self.first, self.last):
+            self.to_right[u].wait_recv()
+            self.far.append(
+                self.mover.go(
+                    self.dst(turn(self.pos, -1), u, 1), self.dst(turn(self.pos, -1), u, 2), right
+                )
+            )
+            self.to_left[v].wait_recv()
+            self.far.append(
+                self.mover.go(
+                    self.dst(turn(self.pos, 1), v, -1), self.dst(turn(self.pos, 1), v, 2), left
+                )
+            )
+
+    def near(self):
+        for u in self.last:
+            self.to_right[u].wait_recv()
+        for v in self.first:
+            self.to_left[v].wait_recv()
+
+    def end(self):
+        for copy in self.far:
+            copy.wait_recv()
+
+
+class Spread:
+    def __init__(self, at, mover, live_out, full, first, width):
+        self.at, self.mover, self.full = at, mover, full
+        self.quarter = width // 4
+        rows = pl.ds(pl.multiple_of(at.c * 16, 16), 16)
+        self.start = [
+            mover.go(
+                live_out.at[rows, pl.ds(first, width)],
+                full.at[k - 1, at.y, at.x, at.core],
+                at.up(turn(at.z, -k)),
+            )
+            for k in range(1, 4)
+        ]
+
+    def cols(self, u, n=1):
+        return pl.ds(u * self.quarter, n * self.quarter)
+
+    def phase_one(self):
+        at, full = self.at, self.full
+        for copy in self.start:
+            copy.wait_recv()
+        a = lambda pos, u, k=0: full.at[:, at.y, pos, at.core, :, self.cols(u)]
+        b = lambda pos, u, k=0: full.at[:, pos, at.x, at.core, :, self.cols(u)]
+        self.one = [
+            Ring(self.mover, at.x, lambda p: at.chip(at.y, p), lambda u: a(at.x, u), a, [0, 1]),
+            Ring(self.mover, at.y, lambda p: at.chip(p, at.x), lambda u: b(at.y, u), b, [2, 3]),
+        ]
+
+    def phase_one_onward(self):
+        for ring in self.one:
+            ring.onward()
+
+    def phase_two(self):
+        at, full = self.at, self.full
+        for ring in self.one:
+            ring.near()
+            ring.end()
+        a = lambda pos, u, k=0: full.at[:, pos, :, at.core, :, self.cols(u)]
+        b = lambda pos, u, k=0: full.at[:, :, pos, at.core, :, self.cols(u)]
+        self.two = [
+            Ring(self.mover, at.y, lambda p: at.chip(p, at.x), lambda u: a(at.y, u), a, [0, 1]),
+            Ring(self.mover, at.x, lambda p: at.chip(at.y, p), lambda u: b(at.x, u), b, [2, 3]),
+        ]
+        self.over = []
+        self.cross(0)
+
+    def cross(self, k):
+        at, full = self.at, self.full
+        a = full.at[:, turn(at.y, k), :, at.core, :, self.cols(0, 2)]
+        b = full.at[:, :, turn(at.x, k), at.core, :, self.cols(2, 2)]
+        for view in (a, b):
+            self.over.append(self.mover.go(view, view, at.sibling()))
+
+    def phase_two_onward(self):
+        for ring in self.two:
+            ring.onward()
+        for ring in self.two:
+            ring.near()
+        self.cross(1)
+        self.cross(-1)
+
+    def finish(self):
+        for ring in self.two:
+            ring.end()
+        self.cross(2)
+        for copy in self.over:
+            copy.wait_recv()
+
+
+def index_kernel(mine, every, send, recv, send2, recv2):
+    at = Place()
+    every[at.c, at.z] = mine[...]
+    greet_all(at)
+    mover = Mover(send, recv)
+    near = [
+        mover.go(every.at[at.c, at.z], every.at[at.c, at.z], at.up(turn(at.z, k)))
+        for k in range(1, 4)
+    ]
+    for copy in near:
+        copy.wait_recv()
+
+    def copy(d):
+        return pltpu.make_async_remote_copy(
+            src_ref=every.at[at.c], dst_ref=every.at[at.c], send_sem=send2.at[d],
+            recv_sem=recv2.at[d], device_id=at.cache(lax.rem(at.c + d, 32)), device_id_type=MESH,
+        )
+
+    def go(d, carry):
+        copy(d).start()
+        return carry
+
+    def wait(d, carry):
+        copy(d).wait()
+        return carry
+
+    lax.fori_loop(1, 32, go, 0)
+    lax.fori_loop(1, 32, wait, 0)
+    mover.finish_sends()
+
+
+def index_exchange(ints):
+    return pl.pallas_call(
+        index_kernel,
+        out_shape=jax.ShapeDtypeStruct((32, 4, 1, 128), jnp.int32),
+        in_specs=[VM],
+        out_specs=VM,
+        scratch_shapes=[
+            pltpu.SemaphoreType.DMA((4,)), pltpu.SemaphoreType.DMA((4,)),
+            pltpu.SemaphoreType.DMA((32,)), pltpu.SemaphoreType.DMA((32,)),
+        ],
+        compiler_params=params(1, 8),
+    )(ints)
+
+
+def fetch_kernel(
+    asked, place, memory, tok, score, live_out,
+    x_full, tokens, scores, full,
+    out_buf, in_buf0, in_buf1, own, pair_buf, a_buf, b_buf, a2_buf, b2_buf, tok_sum,
+    send, recv, a2a_send, a2a_recv, local_sem,
+):
+    at = Place()
+    greet_all(at)
+    mover = Mover(send, recv)
+    spread = Spread(at, mover, live_out, full, 0, 2048)
+    in_buf = (in_buf0, in_buf1)
+
+    def passage_copy(h, d):
+        q = lax.rem(at.c + d, 32)
+        return pltpu.make_async_remote_copy(
+            src_ref=out_buf.at[h, pl.ds(2 * q, 2)], dst_ref=in_buf[h].at[pl.ds(2 * at.c, 2)],
+            send_sem=a2a_send.at[h, d], recv_sem=a2a_recv.at[h, d],
+            device_id=at.cache(q), device_id_type=MESH,
+        )
+
+    def send_half(h):
+        lanes = pl.ds(h * 512, 512)
+
+        def one(d, carry):
+            q = lax.rem(at.c + d, 32)
+            out_buf[h, 2 * q] = memory[asked[2 * q], :, lanes]
+            out_buf[h, 2 * q + 1] = memory[asked[2 * q + 1], :, lanes]
+            passage_copy(h, d).start()
+            return carry
+
+        lax.fori_loop(1, 32, one, 0)
+        in_buf[h][2 * at.c] = memory[asked[2 * at.c], :, lanes]
+        in_buf[h][2 * at.c + 1] = memory[asked[2 * at.c + 1], :, lanes]
+
+    def wait_half(h):
+        def one(d, carry):
+            passage_copy(h, d).wait_recv()
+            return carry
+
+        lax.fori_loop(1, 32, one, 0)
+
+        def pack(j, carry):
+            own[h, pl.ds(pl.multiple_of(16 * j, 16), 16)] = in_buf[h][place[j]]
+            return carry
+
+        lax.fori_loop(0, 32, pack, 0)
+
+    def part(pos, unit, k=0):
+        h, g = unit
+        return x_full.at[
+            pl.ds(g * 256, 256), pl.ds(pl.multiple_of(pos * 1024 + h * 512, 512), 512)
+        ]
+
+    def ring_half(h):
+        keep = pltpu.make_async_copy(
+            own.at[h], x_full.at[:, pl.ds(pl.multiple_of(at.z * 1024 + h * 512, 512), 512)],
+            local_sem.at[h],
+        )
+        keep.start()
+        ring = Ring(
+            mover, at.z, at.up, lambda u: own.at[u[0], pl.ds(u[1] * 256, 256)], part,
+            [(h, 0), (h, 1)],
+        )
+        return ring, keep
+
+    send_half(0)
+    other = 1 - at.core
+    pair = mover.go(tok.at[:, :, other], pair_buf, at.sibling())
+    send_half(1)
+
+    pair.wait_recv()
+
+    def add_pair(y, carry):
+        for x in range(4):
+            pair_buf[y, x] = pair_buf[y, x] + tok[y, x, at.core]
+        return carry
+
+    lax.fori_loop(0, 4, add_pair, 0)
+    lo, hi = pl.ds(0, 512), pl.ds(512, 512)
+    tok_a = [
+        mover.go(
+            pair_buf.at[:, turn(at.x, k), :, lo], a_buf.at[k - 1], at.chip(at.y, turn(at.x, k))
+        )
+        for k in range(1, 4)
+    ]
+    tok_b = [
+        mover.go(
+            pair_buf.at[turn(at.y, k), :, :, hi], b_buf.at[k - 1], at.chip(turn(at.y, k), at.x)
+        )
+        for k in range(1, 4)
+    ]
+    near_scores = [
+        mover.go(score, scores.at[at.z], at.up(turn(at.z, k))) for k in range(1, 4)
+    ]
+    scores[at.z] = score[...]
+    spread.phase_one()
+
+    wait_half(0)
+    ring0, keep0 = ring_half(0)
+    for copy in tok_a + tok_b:
+        copy.wait_recv()
+
+    def add_line(i, carry):
+        a_buf[0, i] = (a_buf[0, i] + a_buf[1, i]) + (a_buf[2, i] + pair_buf[i, at.x, :, lo])
+        b_buf[0, i] = (b_buf[0, i] + b_buf[1, i]) + (b_buf[2, i] + pair_buf[at.y, i, :, hi])
+        return carry
+
+    lax.fori_loop(0, 4, add_line, 0)
+    tok_a2 = [
+        mover.go(a_buf.at[0, turn(at.y, k)], a2_buf.at[k - 1], at.chip(turn(at.y, k), at.x))
+        for k in range(1, 4)
+    ]
+    tok_b2 = [
+        mover.go(b_buf.at[0, turn(at.x, k)], b2_buf.at[k - 1], at.chip(at.y, turn(at.x, k)))
+        for k in range(1, 4)
+    ]
+    wait_half(1)
+    ring1, keep1 = ring_half(1)
+    for copy in tok_a2 + tok_b2:
+        copy.wait_recv()
+    tok_sum[:, lo] = (a2_buf[0] + a2_buf[1]) + (a2_buf[2] + a_buf[0, at.y])
+    tok_sum[:, hi] = (b2_buf[0] + b2_buf[1]) + (b2_buf[2] + b_buf[0, at.x])
+    mine = pl.ds(pl.multiple_of(at.z * 1024, 1024), 1024)
+    near_tokens = [
+        mover.go(tok_sum, tokens.at[:, mine], at.up(turn(at.z, k))) for k in range(1, 4)
+    ]
+    tokens[:, mine] = tok_sum[...]
+    ring0.onward()
+    spread.phase_one_onward()
+    ring1.onward()
+    spread.phase_two()
+    for copy in near_scores + near_tokens:
+        copy.wait_recv()
+    spread.phase_two_onward()
+    for ring in (ring0, ring1):
+        ring.near()
+        ring.end()
+    spread.finish()
+    keep0.wait()
+    keep1.wait()
+    mover.finish_sends()
+
+    def sent(d, carry):
+        passage_copy(0, d).wait_send()
+        passage_copy(1, d).wait_send()
+        return carry
+
+    lax.fori_loop(1, 32, sent, 0)
+
+
+def fetch(asked, place, memory, tok, score, live_out):
+    return pl.pallas_call(
+        fetch_kernel,
+        out_shape=(
+            jax.ShapeDtypeStruct((512, 4096), BF16),
+            jax.ShapeDtypeStruct((48, 4096), BF16),
+            jax.ShapeDtypeStruct((4, 1, 128), F32),
+            jax.ShapeDtypeStruct((3, 4, 4, 2, 16, 2048), BF16),
+        ),
+        in_specs=[SM, SM, VM, VM, VM, ANY],
+        out_specs=(ANY, VM, VM, ANY),
+        scratch_shapes=[
+            pltpu.VMEM((2, 64, 16, 512), BF16), pltpu.VMEM((64, 16, 512), BF16),
+            pltpu.VMEM((64, 16, 512), BF16),
+            pltpu.VMEM((2, 512, 512), BF16), pltpu.VMEM((4, 4, 48, 1024), BF16),
+            pltpu.VMEM((3, 4, 48, 512), BF16), pltpu.VMEM((3, 4, 48, 512), BF16),
+            pltpu.VMEM((3, 48, 512), BF16), pltpu.VMEM((3, 48, 512), BF16),
+            pltpu.VMEM((48, 1024), BF16),
+            pltpu.SemaphoreType.DMA((80,)), pltpu.SemaphoreType.DMA((80,)),
+            pltpu.SemaphoreType.DMA((2, 32)), pltpu.SemaphoreType.DMA((2, 32)),
+            pltpu.SemaphoreType.DMA((2,)),
+        ],
+        compiler_params=params(2, 40),
+    )(asked, place, memory, tok, score, live_out)
+
+
+def context_kernel(ctx, live_out, others, full, send, recv):
+    at = Place()
+    greet_all(at)
+    mover = Mover(send, recv)
+    spread = Spread(at, mover, live_out, full, 2048, 2048)
+    rows = lambda u: pl.ds(u * 256, 256)
+
+    def part(pos, u, k):
+        return others.at[{1: 2, -1: 0, 2: 1}[k], rows(u)]
+
+    ring = Ring(mover, at.z, at.up, lambda u: ctx.at[rows(u)], part, [0, 1, 2, 3])
+    spread.phase_one()
+    spread.phase_one_onward()
+    ring.onward()
+    spread.phase_two()
+    spread.phase_two_onward()
+    ring.near()
+    ring.end()
+    spread.finish()
+    mover.finish_sends()
+
+
+def share_context(ctx, live_out):
+    return pl.pallas_call(
+        context_kernel,
+        out_shape=(
+            jax.ShapeDtypeStruct((3, 1024, 512), BF16),
+            jax.ShapeDtypeStruct((3, 4, 4, 2, 16, 2048), BF16),
+        ),
+        in_specs=[ANY, ANY],
+        out_specs=(ANY, ANY),
+        scratch_shapes=[pltpu.SemaphoreType.DMA((64,)), pltpu.SemaphoreType.DMA((64,))],
+        compiler_params=params(3, 8),
+    )(ctx, live_out)
+
+
+def greet_z(at):
+    barrier = pltpu.get_barrier_semaphore()
+    for k in range(1, 4):
+        pl.semaphore_signal(barrier, inc=1, device_id=at.up(turn(at.z, k)), device_id_type=MESH)
+    pl.semaphore_wait(barrier, 3)
+
+
+def inverse_kernel(mine, every, send, recv):
+    at = Place()
+    every[at.z] = mine[...]
+    greet_z(at)
+    mover = Mover(send, recv)
+    near = [mover.go(mine, every.at[at.z], at.up(turn(at.z, k))) for k in range(1, 4)]
+    for copy in near:
+        copy.wait_recv()
+    mover.finish_sends()
+
+
+def share_inverse(mine):
+    return pl.pallas_call(
+        inverse_kernel,
+        out_shape=jax.ShapeDtypeStruct((4, 2, 128), F32),
+        in_specs=[VM],
+        out_specs=VM,
+        scratch_shapes=[pltpu.SemaphoreType.DMA((4,)), pltpu.SemaphoreType.DMA((4,))],
+        compiler_params=params(4, 4),
+    )(mine)
+
+
+def decoded_kernel(part, out, buf, send, recv):
+    at = Place()
+    greet_z(at)
+    mover = Mover(send, recv)
+    near = [
+        mover.go(part.at[turn(at.z, k)], buf.at[k - 1], at.up(turn(at.z, k)))
+        for k in range(1, 4)
+    ]
+    for copy in near:
+        copy.wait_recv()
+    total = part[at.z].astype(F32)
+    for k in range(3):
+        total = total + buf[k].astype(F32)
+    out[...] = total.astype(BF16)
+    mover.finish_sends()
+
+
+def add_decoded(part):
+    return pl.pallas_call(
+        decoded_kernel,
+        out_shape=jax.ShapeDtypeStruct((32, 1024), BF16),
+        in_specs=[VM],
+        out_specs=VM,
+        scratch_shapes=[
+            pltpu.VMEM((3, 32, 1024), BF16),
+            pltpu.SemaphoreType.DMA((4,)), pltpu.SemaphoreType.DMA((4,)),
+        ],
+        compiler_params=params(5, 8),
+    )(part)
 
 
 def shards(
@@ -73,18 +574,13 @@
     cols = live_out.shape[0]
     scale = HEAD ** (-0.5)
 
-    piece_rows = cols // n_cache
-    piece = lax.dynamic_slice_in_dim(live_out, me_c * piece_rows, piece_rows, 0)
-    pieces = lax.all_gather(piece, "psg", axis=0, tiled=False)
-    out_full = [lax.all_gather(pieces[z], "cache", axis=0, tiled=True) for z in range(n_psg)]
-
     ints = jnp.concatenate(
-        [question_ids[0], answer_ids[0], owner[0, :, 0], slot[0]], axis=0
-    ).reshape(1, 1, -1)
-    every = lax.all_gather(ints, ("cache", "psg"), axis=0, tiled=True).reshape(n_cache, n_psg, -1)
+        [question_ids[0], answer_ids[0], owner[0, :, 0], slot[0], jnp.zeros((64,), jnp.int32)]
+    ).reshape(1, 128)
+    every = index_exchange(ints).reshape(n_cache, n_psg, 128)
     tokens = every[:, 0, : qlen + alen]
     owners = every[:, :, qlen + alen : qlen + alen + own_count].reshape(n_cache, total)
-    slots = every[:, :, qlen + alen + own_count :].reshape(n_cache, total)
+    slots = every[:, :, qlen + alen + own_count : 64].reshape(n_cache, total)
     order = jnp.arange(total)
     earlier = (owners[:, :, None] == owners[:, None, :]) & (order[None, :] < order[:, None])[None]
     rank = jnp.sum(earlier, axis=2)
@@ -93,52 +589,58 @@
         jnp.where(mine[:, None, :] & (rank[:, None, :] == jnp.arange(2)[None, :, None]),
                   slots[:, None, :], 0),
         axis=2,
-    )
+    ).reshape(-1)
     place = lax.dynamic_index_in_dim(owners * 2 + rank, me_c, 0, False)
-    looked_up = jnp.take(memory, asked.reshape(-1), axis=0).reshape((n_cache, 2) + memory.shape[1:])
-    fetched = lax.all_to_all(looked_up, "cache", split_axis=0, concat_axis=0, tiled=True)
-    slices = jnp.take(fetched.reshape((-1,) + memory.shape[1:]), place, axis=0)
-    x_mem = lax.all_gather(slices, "psg", axis=2, tiled=True).reshape(total * plen, width)
-
     vocab = embedding.shape[0]
     onehot = (
         (tokens - me_c * vocab)[:, :, None] == jnp.arange(vocab, dtype=jnp.int32)
     ).astype(BF16)
-    token_slice = lax.psum_scatter(
-        jnp.einsum("qtv,vf->qtf", onehot, embedding, preferred_element_type=F32).astype(BF16),
-        "cache", scatter_dimension=0, tiled=True,
+    tok = jnp.einsum("qtv,vf->qtf", onehot, embedding, preferred_element_type=F32).astype(BF16)
+    score = jnp.pad(passage_score, ((0, 0), (0, 120)))
+    x_mem, token_full, scores, full_left = fetch(
+        asked, place, memory, tok.reshape(4, 4, 2, qlen + alen, -1), score, live_out
     )
-    token_full = lax.all_gather(token_slice, "psg", axis=2, tiled=True)[0]
     x_q = token_full[:qlen]
     answer = token_full[qlen:]
-    score_all = lax.all_gather(passage_score[0], "psg", axis=0, tiled=True)
+    score_all = scores[:, 0, :own_count].reshape(total)
 
     q_dec = norm_project(answer, dec_gain, cross_query).reshape(alen, heads, HEAD)
-    w_key = cross_kv[:, 0].reshape(width, heads, HEAD)
-    w_val = cross_kv[:, 1].reshape(width, heads, HEAD)
+    kv = cross_kv.reshape(width, 2 * cols)
+    w_key = kv[:, :cols].reshape(width, heads, HEAD)
+    w_val = kv[:, cols:].reshape(width, heads, HEAD)
     qg = (
         jnp.einsum("thd,fhd->htf", q_dec, w_key, preferred_element_type=F32) * enc_gain
     ).astype(BF16).reshape(heads * alen, width)
-    ql = [dot32(qg, o, ((1,), (1,))).astype(BF16) for o in out_full]
-
-    w_qkv = live_qkv.reshape(width, 3 * cols)
-    mem_proj = norm_project(x_mem, live_gain, w_qkv).reshape(total, plen, 3 * cols)
-    q_proj = norm_project(x_q, live_gain, w_qkv)
-    proj = jnp.concatenate(
-        [mem_proj, jnp.broadcast_to(q_proj[None], (total, qlen, 3 * cols))], axis=1
-    ).reshape(total, seq, 3, heads, HEAD)
+
+    proj = []
+    for i in range(3):
+        w = live_qkv[:, i]
+        m = norm_project(x_mem, live_gain, w).reshape(total, plen, cols)
+        n = norm_project(x_q, live_gain, w)
+        proj.append(
+            jnp.concatenate([m, jnp.broadcast_to(n[None], (total, qlen, cols))], axis=1).reshape(
+                total, seq, heads, HEAD
+            )
+        )
     scores = jnp.einsum(
-        "pqhd,pkhd->phqk", proj[:, :, 0], proj[:, :, 1], preferred_element_type=F32
+        "pqhd,pkhd->phqk", proj[0], proj[1], preferred_element_type=F32
     ) * scale + position_bias(rel_bias, seq)[None]
     ctx = (
-        jnp.einsum("phqk,pkhd->pqhd", softmax_rows(scores), proj[:, :, 2],
+        jnp.einsum("phqk,pkhd->pqhd", softmax_rows(scores), proj[2],
                    preferred_element_type=F32)
         .astype(BF16).reshape(total * seq, cols)
     )
-    ctx_all = lax.all_gather(ctx, "psg", axis=0, tiled=False)
+    others, full_right = share_context(ctx, live_out)
+    ctx_all = [ctx] + [others[k] for k in range(3)]
+    full_left = full_left.reshape(3, cols, width // 2)
+    full_right = full_right.reshape(3, cols, width // 2)
+    out_full = [live_out] + [
+        jnp.concatenate([full_left[k], full_right[k]], axis=1) for k in range(3)
+    ]
+    ql = [dot32(qg, o, ((1,), (1,))).astype(BF16) for o in out_full]
 
     own_rows = own_count * seq
-    own_ctx = lax.dynamic_slice_in_dim(ctx_all, me_z * own_rows, own_rows, 1)
+    own_ctx = [lax.dynamic_slice_in_dim(c, me_z * own_rows, own_rows, 0) for c in ctx_all]
     attended = sum(
         dot32(own_ctx[z], out_full[z], ((1,), (0,))).astype(BF16).astype(F32) for z in range(n_psg)
     )
@@ -150,7 +652,7 @@
     encoded = (own_input.astype(F32) + attended).astype(BF16)
     enc32 = encoded.astype(F32)
     inv_own = lax.rsqrt(jnp.mean(enc32 * enc32, axis=-1) + EPSILON)
-    inv = lax.all_gather(inv_own, "psg", axis=0, tiled=True)
+    inv = share_inverse(inv_own.reshape(2, 128)).reshape(total * seq)
 
     s_mem = dot32(qg, x_mem, ((1,), (1,))).reshape(-1, total, plen)
     s_q = jnp.broadcast_to(dot32(qg, x_q, ((1,), (1,)))[:, None], (heads * alen, total, qlen))
@@ -171,10 +673,8 @@
         zed = zed + dot32(part, out_full[z], ((1,), (0,)))
     zed = (zed * enc_gain).astype(BF16).reshape(heads, alen, width)
     context = jnp.einsum("htf,fhd->thd", zed, w_val, preferred_element_type=F32).astype(BF16)
-    decoded = lax.psum_scatter(
-        dot32(context.reshape(alen, -1), cross_out, ((1,), (0,))).astype(BF16),
-        "psg", scatter_dimension=1, tiled=True,
-    )
+    part = dot32(context.reshape(alen, -1), cross_out, ((1,), (0,))).astype(BF16)
+    decoded = add_decoded(part.reshape(alen, n_psg, -1).transpose(1, 0, 2))
     return encoded.reshape(1, own_count, seq, width), decoded[None]
 
 

time: 532 us -> 353 us (0.66)
  Pallas kernels: 0 us -> 147 us
  waiting for transfers between devices: 144 us -> 0 us
  blocking collectives: 111 us -> 0 us
  local copies, waits for them, and re-layouts: 106 us -> 64.2 us
  between operations: 16.9 us -> 1.49 us
  starting transfers between devices: 5.5 us -> 0 us
    pallas_call x0 -> x5, Pallas kernels: none -> 147 us  [the longest x1 74.7 us: fetch(): pl.pallas_call(fetch_kernel, out_shape=(jax.ShapeDtypeStruct((512, 4096),...]
    all_gather x6 -> x0, waiting for transfers between devices: 97 us -> none  [the longest x4 97 us: shards(): lax.all_gather(pieces[z], 'cache', axis=0, tiled=True)]
    unnamed x2 -> x0, blocking collectives: 78.5 us -> none
    slice x5 -> x7, local copies, waits for them, and re-layouts: 55.1 us -> 15.3 us  [the longest x1 5.43 us: shards(): w_val = kv[:, cols:].reshape(width, heads, HEAD)]
    all_gather x3 -> x0, blocking collectives: 32.8 us -> none  [the longest x1 13.1 us: shards(): token_full = lax.all_gather(token_slice, 'psg', axis=2, tiled=True)[0]]
    all_to_all x1 -> x0, waiting for transfers between devices: 27.9 us -> none  [shards(): lax.all_to_all(looked_up, 'cache', split_axis=0, concat_axis=0, tiled=True)]
    reshape x2 -> x4, local copies, waits for them, and re-layouts: 0.2 us -> 24.6 us  [the longest x1 21.2 us: shards(): kv = cross_kv.reshape(width, 2 * cols)]
    reduce_scatter x2 -> x0, waiting for transfers between devices: 17.4 us -> none  [the longest x1 17.3 us: shards(): lax.psum_scatter(dot32(context.reshape(alen, -1), cross_out, ((1,), (0,))...]
  transfers between devices with their start and end apart: 9 -> 0, of which waited for: 5 -> 0; matrix products, arithmetic and copies ran while one was open for 32% -> 0% of each run, Pallas kernels for 0% -> 0%
where the time goes in v2:
time: 353 us; the launch traced here: 346 us
  Pallas kernels  147 us (42%)
  matrix products  120 us (34%)
  local copies, waits for them, and re-layouts  64.2 us (18%)
  other arithmetic  13 us (4%)
    dot_general x17, matrix products, dot32(): return lax.dot_general(a, b, (dims, ((), ())), preferred_element_type=F32)  78.3 us
    pallas_call x1, Pallas kernels, fetch(): pl.pallas_call(fetch_kernel, out_shape=(jax.ShapeDtypeStruct((512, 4096),...  74.7 us
    pallas_call x1, Pallas kernels, share_context(): pl.pallas_call(context_kernel, out_shape=(jax.ShapeDtypeStruct((3, 1024,...  46.1 us
    dot_general x7, matrix products, norm_project(): projected = jnp.dot(scaled, weights, preferred_element_type=F32)  25.3 us
    reshape x1, local copies, waits for them, and re-layouts, shards(): kv = cross_kv.reshape(width, 2 * cols)  21.2 us
    pallas_call x1, Pallas kernels, index_exchange(): pl.pallas_call(index_kernel, out_shape=jax.ShapeDtypeStruct((32, 4, 1, 12...  16.9 us
    unnamed x53, local copies, waits for them, and re-layouts  10.5 us
    sub x1, other arithmetic, softmax_rows(): exponents = jnp.exp(scores - maximum)  7.07 us

profile of v2, /device:TPU:1, one launch (start us, length us, event | category | flops | bytes accessed | tf_op | source)
XLA Modules:
  0.0 346.3 jit_solution(3787160743856858273)
XLA Ops:
  1.6 16.9 %shard_map.176 = s32[32,4,1,128]{3,2,1,0:T(1,128)S(1)} custom-call(s32[1,128]{1,0:T(1,128)S(1)} %bitcast.160), custom_call_target="tpu_custom_call" | custom-call | tf_op jit(solution)/shard_map/pallas_call | solution.py:273
  20.3 3.7 %fusion.41 = bf16[32,48,1024]{2,1,0:T(8,128)(2,1)S(1)} fusion(s32[32,48]{1,0:T(8,128)S(1)} %bitcast.199, bf16[1004,1024]{1,0:T(8,128)(2,1)S(1)} %copy-done), kind=kOutput, calls=%fused_computation.59 | convolution fusion | flops 3161425920 | bytes 5208064 | tf_op jit(solution)/shard_map/qtv,vf->qtf/dot_general | solution.py:598
  24.1 74.7 %shard_map.177 = (bf16[512,4096]{1,0:T(8,128)(2,1)S(1)}, bf16[48,4096]{1,0:T(8,128)(2,1)S(1)}, f32[4,1,128]{2,1,0:T(1,128)S(1)}, bf16[3,4,4,2,16,2048]{5,4,3,2,1,0:T(8,128)(2,1)}) custom-call(s32[64]{0:T(128)S(1)} %reshape.190.asked, s32[32]{0:T(128)S(1)} %fusion.152.place, bf16[32,16,1024]{2,1,0:T(8,128)(2,1)S(1)} %copy-done.8, ...), custom_call_target="tpu_custom_call" | custom-call | tf_op jit(solution)/shard_map/pallas_call | solution.py:437
  98.8 2.0 copy-done.4
  102.0 21.2 %copy.134 = bf16[4096,2,512]{0,2,1:T(8,128)(2,1)} copy(bf16[4096,2,512]{2,1,0:T(2,128)(2,1)} %param.29) | data formatting | bytes 16777216 | tf_op jit(solution)/shard_map/reshape | solution.py:608
  123.2 5.4 %fusion.183 = (bf16[4096,512]{0,1:T(8,128)(2,1)}, bf16[4096,512]{0,1:T(8,128)(2,1)S(1)}) fusion(bf16[4096,1024]{0,1:T(8,128)(2,1)} %bitcast.161), kind=kLoop, calls=%fused_computation.188 | loop fusion | bytes 16777216 | tf_op jit(solution)/shard_map/slice | solution.py:610
  130.1 1.5 copy-done.5
  131.6 3.1 fusion.28
  135.5 1.3 copy.128
  137.0 2.8 fusion.108
  140.2 2.8 fusion.111
  143.1 1.2 broadcast_in_dim.44
  144.3 3.5 %fusion.2 = f32[512]{0:T(512)S(1)} fusion(bf16[512,4096]{1,0:T(8,128)(2,1)} %copy-done.4), kind=kLoop, calls=%fused_computation.4 | loop fusion | flops 6290944 | bytes 4196352 | tf_op jit(solution)/shard_map/reduce_sum | solution.py:45
  147.8 4.5 %fusion.76 = bf16[512,512]{1,0:T(8,128)(2,1)S(1)} fusion(bf16[4096,3,512]{2,0,1:T(8,128)(2,1)} %param.25, bf16[512,4096]{1,0:T(8,128)(2,1)S(1)} %copy-done.6, f32[4096]{0:T(1024)S(1)} %copy-done.21, f32[512]{0:T(512)S(1)} %add_rsqrt_fusion), kind=kOutput, calls=%fused_computation.86 | convolution fusion | flops 2154299392 | bytes 8931328 | tf_op jit(solution)/shard_map/dot_general | solution.py:47
  152.9 1.2 copy.120
  154.1 5.8 %fusion.81 = bf16[512,512]{1,0:T(8,128)(2,1)S(1)} fusion(bf16[4096,3,512]{2,0,1:T(8,128)(2,1)} %param.25, bf16[512,4096]{1,0:T(8,128)(2,1)} %copy-done.4, f32[4096]{0:T(1024)S(1)} %copy-done.21, f32[512]{0:T(512)S(1)} %add_rsqrt_fusion), kind=kOutput, calls=%fused_computation.87 | convolution fusion | flops 2154299392 | bytes 8931328 | tf_op jit(solution)/shard_map/dot_general | solution.py:47
  160.9 4.8 %fusion.46 = f32[32,8,32,32]{2,3,1,0:T(8,128)} fusion(bf16[32,16,8,64]{3,1,2,0:T(8,128)(2,1)} %broadcast_in_dim.44, bf16[32,16,8,64]{3,1,2,0:T(8,128)(2,1)S(1)} %copy.118, bf16[32,16,8,64]{3,1,2,0:T(8,128)(2,1)S(1)} %broadcast_in_dim.46, bf16[32,16,8,64]{3,1,2,0:T(8,128)(2,1)} %copy.120), kind=kOutput, calls=%fused_computation.65 | convolution fusion | flops 37748736 | bytes 3145728 | tf_op jit(solution)/shard_map/pqhd,pkhd->phqk/dot_general | solution.py:625
  166.1 7.1 %fusion.188 = (f32[32,8,32]{2,1,0:T(8,128)S(1)}, f32[32,8,32,32]{2,3,1,0:T(8,128)}) fusion(f32[32,8,32,32]{2,3,1,0:T(8,128)} %fusion.46, f32[8,32,32]{1,2,0:T(8,128)S(1)} %copy.121), kind=kOutput, calls=%fused_computation.193 | output fusion | flops 1572895 | bytes 2162688 | tf_op jit(solution)/shard_map/sub | solution.py:53
  173.2 2.8 fusion.114
  176.3 5.8 %fusion.86 = bf16[512,512]{1,0:T(8,128)(2,1)S(1)} fusion(bf16[4096,3,512]{2,0,1:T(8,128)(2,1)} %param.25, bf16[512,4096]{1,0:T(8,128)(2,1)} %copy-done.4, f32[4096]{0:T(1024)S(1)} %copy-done.21, f32[512]{0:T(512)S(1)} %add_rsqrt_fusion), kind=kOutput, calls=%fused_computation.88 | convolution fusion | flops 2154299392 | bytes 8931328 | tf_op jit(solution)/shard_map/dot_general | solution.py:47
  182.9 3.2 convert_bitcast_fusion
  186.1 2.3 copy.123
  188.5 3.2 reshape.193.ctx
  191.7 5.4 %convolution_add_fusion.8 = f32[256,1024]{1,0:T(8,128)} fusion(f32[256,1024]{1,0:T(8,128)S(1)} %copy-done.16, bf16[1024,512]{1,0:T(8,128)(2,1)S(1)} %reshape.193.ctx, bf16[256,4096]{1,0:T(8,128)(2,1)} %bitcast.178, bf16[512,4096]{1,0:T(8,128)(2,1)} %live_out.3), kind=kOutput, calls=%fused_computation.82 | convolution fusion | flops 1342570496 | bytes 9437184 | tf_op jit(solution)/shard_map/dot_general | solution.py:58
  197.1 2.2 copy-done.3
  199.3 46.1 %shard_map.178 = (bf16[3,1024,512]{2,1,0:T(8,128)(2,1)S(1)}, bf16[3,4,4,2,16,2048]{5,4,3,2,1,0:T(8,128)(2,1)S(1)}) custom-call(bf16[1024,512]{1,0:T(8,128)(2,1)S(1)} %reshape.193.ctx, bf16[512,4096]{1,0:T(8,128)(2,1)S(1)} %copy-done.3), custom_call_target="tpu_custom_call" | custom-call | tf_op jit(solution)/shard_map/pallas_call | solution.py:485
  245.4 1.7 copy-done.7
  247.0 3.4 fusion.185
  252.1 2.9 fusion.184
  255.0 5.7 %convolution_add_fusion.7 = f32[256,1024]{1,0:T(8,128)} fusion(f32[256,1024]{1,0:T(8,128)S(1)} %copy-done.23, bf16[256,4096]{1,0:T(8,128)(2,1)} %bitcast.179, bf16[512,2048]{1,0:T(8,128)(2,1)} %bitcast.165, bf16[512,2048]{1,0:T(8,128)(2,1)} %bitcast.171, bf16[3,1024,512]{2,1,0:T(8,128)(2,1)} %copy-done.7), kind=kOutput, calls=%fused_computation.81 | convolution fusion | flops 1350959104 | bytes 9437184 | tf_op jit(solution)/shard_map/dot_general | solution.py:58
  260.7 6.0 %convolution_add_fusion.6 = f32[256,1024]{1,0:T(8,128)} fusion(f32[256,1024]{1,0:T(8,128)} %convolution_add_fusion.7, bf16[256,4096]{1,0:T(8,128)(2,1)} %bitcast.180, bf16[512,2048]{1,0:T(8,128)(2,1)} %bitcast.162, bf16[512,2048]{1,0:T(8,128)(2,1)} %bitcast.168, bf16[3,1024,512]{2,1,0:T(8,128)(2,1)} %copy-done.7), kind=kOutput, calls=%fused_computation.80 | convolution fusion | flops 1350959104 | bytes 9437184 | tf_op jit(solution)/shard_map/dot_general | solution.py:58
  266.8 3.4 fusion.186
  270.2 3.6 %fusion.15 = f32[256,4096]{1,0:T(8,128)S(1)} fusion(bf16[512,4096]{1,0:T(8,128)(2,1)} %live_out.3, bf16[1024,512]{1,0:T(8,128)(2,1)S(1)} %reshape.193.ctx, s32[]{:T(128)S(6)} %select_n.20), kind=kOutput, calls=%fused_computation.28 | convolution fusion | flops 1075838976 | bytes 8650756 | tf_op jit(solution)/shard_map/dot_general | solution.py:58
  273.9 2.5 fusion.14
  276.4 3.3 fusion.12
  279.8 1.5 constant_dynamic-slice_fusion
  282.3 5.2 %multiply_reduce_fusion = (f32[256]{0:T(256)S(1)}, bf16[256,4096]{1,0:T(8,128)(2,1)}) fusion(f32[256,4096]{1,0:T(8,128)S(1)} %copy-done.15, bf16[512,2048]{1,0:T(8,128)(2,1)} %bitcast.189, bf16[512,2048]{1,0:T(8,128)(2,1)} %bitcast.192, bf16[1,1024,512]{2,1,0:T(8,128)(2,1)} %get-tuple-element.22, s32[]{:T(128)S(6)} %select_n.20, ...), kind=kOutput, calls=%fused_computation.47 | convolution fusion | flops 1091567360 | bytes 12846084 | tf_op jit(solution)/shard_map/dot_general | solution.py:58
  287.5 4.0 %shard_map.179 = f32[4,2,128]{2,1,0:T(2,128)S(1)} custom-call(f32[2,128]{1,0:T(2,128)S(1)} %rsqrt_bitcast_fusion.mine), custom_call_target="tpu_custom_call" | custom-call | tf_op jit(solution)/shard_map/pallas_call | solution.py:517
  291.8 5.2 %fusion.189 = (f32[256]{0:T(256)S(1)}, f32[256,1024]{1,0:T(8,128)S(1)}) fusion(f32[1024]{0:T(1024)S(1)} %add.137, f32[1024]{0:T(1024)S(1)} %broadcast_multiply_fusion, f32[256,1024]{1,0:T(8,128)} %convolution_add_fusion.6, bf16[3,1024,512]{2,1,0:T(8,128)(2,1)} %copy-done.7, bf16[256,4096]{1,0:T(8,128)(2,1)} %bitcast.181, bf16[512,2048]{1,0:T(8,128)(2,1)} %bitcast.190, ...), kind=kOutput, calls=%fused_computation.194 | convolution fusion | flops 1351745280 | bytes 9446400 | tf_op jit(solution)/shard_map/dot_general | solution.py:58
  298.0 3.5 %fusion.190 = f32[256,4096]{1,0:T(8,128)S(1)} fusion(bf16[256,512]{0,1:T(8,128)(2,1)S(1)} %bitcast.195, bf16[512,4096]{1,0:T(8,128)(2,1)} %copy-done.4), kind=kOutput, calls=%fused_computation.195 | convolution fusion | flops 1073741824 | bytes 8650752 | tf_op jit(solution)/shard_map/dot_general | solution.py:58
  301.5 2.7 convolution_add_fusion.4
  304.1 7.0 %convolution_add_fusion.3 = f32[256,4096]{1,0:T(8,128)} fusion(f32[256,4096]{1,0:T(8,128)} %convolution_add_fusion.4, bf16[512,4096]{1,0:T(8,128)(2,1)} %live_out.3, bf16[256,1024]{1,0:T(8,128)(2,1)S(1)} %divide_convert_fusion.4, bf16[1024,512]{1,0:T(8,128)(2,1)S(1)} %reshape.193.ctx), kind=kOutput, calls=%fused_computation.11 | convolution fusion | flops 1343356928 | bytes 14155776 | tf_op jit(solution)/shard_map/dot_general | solution.py:58
  311.2 7.4 %convolution_add_fusion.2 = f32[256,4096]{1,0:T(8,128)} fusion(f32[256,4096]{1,0:T(8,128)} %convolution_add_fusion.3, bf16[512,2048]{1,0:T(8,128)(2,1)} %bitcast.166, bf16[512,2048]{1,0:T(8,128)(2,1)} %bitcast.172, bf16[256,1024]{1,0:T(8,128)(2,1)S(1)} %divide_convert_fusion.4, bf16[3,1024,512]{2,1,0:T(8,128)(2,1)} %copy-done.7), kind=kOutput, calls=%fused_computation.10 | convolution fusion | flops 1351745536 | bytes 14155776 | tf_op jit(solution)/shard_map/dot_general | solution.py:58
  318.5 7.4 %convolution_add_fusion.1 = f32[256,4096]{1,0:T(8,128)} fusion(f32[256,4096]{1,0:T(8,128)} %convolution_add_fusion.2, bf16[512,2048]{1,0:T(8,128)(2,1)} %bitcast.163, bf16[512,2048]{1,0:T(8,128)(2,1)} %bitcast.169, bf16[256,1024]{1,0:T(8,128)(2,1)S(1)} %divide_convert_fusion.4, bf16[3,1024,512]{2,1,0:T(8,128)(2,1)} %copy-done.7), kind=kOutput, calls=%fused_computation.9 | convolution fusion | flops 1351745536 | bytes 14155776 | tf_op jit(solution)/shard_map/dot_general | solution.py:58
  325.9 6.7 %fusion.5 = bf16[256,4096]{1,0:T(8,128)(2,1)} fusion(f32[256,4096]{1,0:T(8,128)} %convolution_add_fusion.1, f32[4096]{0:T(1024)S(1)} %copy-done.19, bf16[512,2048]{1,0:T(8,128)(2,1)} %bitcast.191, bf16[512,2048]{1,0:T(8,128)(2,1)} %bitcast.194, bf16[256,1024]{1,0:T(8,128)(2,1)S(1)} %divide_convert_fusion.4, bf16[3,1024,512]{2,1,0:T(8,128)(2,1)} %copy-done.7), kind=kOutput, calls=%fused_computation.14 | convolution fusion | flops 1353842688 | bytes 12075008 | tf_op jit(solution)/shard_map/dot_general | solution.py:58
  332.6 4.2 %fusion.97 = bf16[32,8,64]{2,0,1:T(8,128)(2,1)S(1)} fusion(bf16[8,32,4096]{2,1,0:T(8,128)(2,1)} %bitcast.186, bf16[4096,8,64]{0,2,1:T(8,128)(2,1)} %bitcast.174), kind=kOutput, calls=%fused_computation.101 | convolution fusion | flops 134234112 | bytes 6324224 | tf_op jit(solution)/shard_map/htf,fhd->thd/dot_general | solution.py:675
  336.9 3.0 convolution_convert_fusion.4
  340.0 5.5 %shard_map.180 = bf16[32,1024]{1,0:T(8,128)(2,1)S(1)} custom-call(bf16[4,32,1024]{2,1,0:T(8,128)(2,1)S(1)} %bitcast.154), custom_call_target="tpu_custom_call" | custom-call | tf_op jit(solution)/shard_map/pallas_call | solution.py:545
  (111 shorter events, 14.5 us)
Async XLA Ops:
  0.6 19.7 %copy-start = (bf16[1004,1024]{1,0:T(8,128)(2,1)S(1)}, bf16[1004,1024]{1,0:T(8,128)(2,1)}, u32[]{:S(2)}) copy-start(bf16[1004,1024]{1,0:T(8,128)(2,1)} %param.23) | copy-start | bytes 6168580
  20.3 3.8 %copy-start.22 = (f32[1,8]{1,0:T(1,128)S(1)}, f32[1,8]{1,0:T(1,128)}, u32[]{:S(2)}) copy-start(f32[1,8]{1,0:T(1,128)} %param.21) | copy-start | bytes 100
  20.3 3.8 %copy-start.2 = (bf16[512,4096]{1,0:T(8,128)(2,1)S(1)}, bf16[512,4096]{1,0:T(8,128)(2,1)}, u32[]{:S(2)}) copy-start(bf16[512,4096]{1,0:T(8,128)(2,1)} %live_out.3) | copy-start | bytes 12582916
  20.3 3.8 %copy-start.8 = (bf16[32,16,1024]{2,1,0:T(8,128)(2,1)S(1)}, bf16[32,16,1024]{2,1,0:T(8,128)(2,1)}, u32[]{:S(2)}) copy-start(bf16[32,16,1024]{2,1,0:T(8,128)(2,1)} %memory.1) | copy-start | bytes 3145732
  24.1 76.9 %copy-start.14 = (bf16[4096,512]{1,0:T(8,128)(2,1)S(1)}, bf16[4096,512]{1,0:T(8,128)(2,1)}, u32[]{:S(2)}) copy-start(bf16[4096,512]{1,0:T(8,128)(2,1)} %param.31) | copy-start | bytes 12582916
  24.1 76.9 %copy-start.18 = (f32[4096]{0:T(1024)S(1)}, f32[4096]{0:T(1024)}, u32[]{:S(2)}) copy-start(f32[4096]{0:T(1024)} %param.30) | copy-start | bytes 49156
  98.8 2.0 copy-start.4
  123.2 5.4 %copy-start.19 = (f32[4096]{0:T(1024)S(1)}, f32[4096]{0:T(1024)}, u32[]{:S(2)}) copy-start(f32[4096]{0:T(1024)} %param.28) | copy-start | bytes 49156
  128.7 2.9 copy-start.5
  129.4 5.3 %copy-start.13 = (bf16[8,32,4096]{2,1,0:T(8,128)(2,1)}, bf16[8,32,4096]{2,1,0:T(8,128)(2,1)S(1)}, u32[]{:S(2)}) copy-start(bf16[8,32,4096]{2,1,0:T(8,128)(2,1)S(1)} %fusion.6) | copy-start | bytes 6291460
  134.7 2.2 copy-start.21
  143.1 4.7 %copy-start.6 = (bf16[512,4096]{1,0:T(8,128)(2,1)S(1)}, bf16[512,4096]{1,0:T(8,128)(2,1)}, u32[]{:S(2)}) copy-start(bf16[512,4096]{1,0:T(8,128)(2,1)} %copy-done.4) | copy-start | bytes 12582916
  160.9 4.8 %copy-start.17 = (f32[32,1024]{1,0:T(8,128)S(1)}, f32[32,1024]{1,0:T(8,128)}, u32[]{:S(2)}) copy-start(f32[32,1024]{1,0:T(8,128)} %constant.60.clone) | copy-start | bytes 393220
  160.9 4.8 %copy-start.20 = (f32[8,32]{1,0:T(8,128)S(1)}, f32[8,32]{1,0:T(8,128)}, u32[]{:S(2)}) copy-start(f32[8,32]{1,0:T(8,128)} %param.26) | copy-start | bytes 3076
  186.1 5.5 %copy-start.16 = (f32[256,1024]{1,0:T(8,128)S(1)}, f32[256,1024]{1,0:T(8,128)}, u32[]{:S(2)}) copy-start(f32[256,1024]{1,0:T(8,128)} %copy.128) | copy-start | bytes 3145732
  197.1 2.2 copy-start.3
  245.4 1.7 copy-start.7
  247.0 4.4 %slice-start = ((s8[6291456]{0:T(1024)(128)(4,1)}), s8[4194304]{0:T(1024)(128)(4,1)S(1)}, s32[]{:S(2)}) async-start(s8[6291456]{0:T(1024)(128)(4,1)} %bitcast.182), calls=%async_computation | async-start | bytes 8388608
  247.0 5.1 %slice-start.1 = ((s8[6291456]{0:T(1024)(128)(4,1)}), s8[2097152]{0:T(1024)(128)(4,1)S(1)}, s32[]{:S(2)}) async-start(s8[6291456]{0:T(1024)(128)(4,1)} %bitcast.182), calls=%async_computation.1 | async-start | bytes 4194304
  252.1 2.9 copy-start.23
  270.2 3.7 %copy-start.10 = (bf16[1,4,4,2,16,2048]{5,4,3,2,1,0:T(8,128)(2,1)S(1)}, bf16[1,4,4,2,16,2048]{5,4,3,2,1,0:T(8,128)(2,1)}, u32[]{:S(2)}) copy-start(bf16[1,4,4,2,16,2048]{5,4,3,2,1,0:T(8,128)(2,1)} %get-tuple-element.21) | copy-start | bytes 6291460
  270.2 3.7 %copy-start.12 = (bf16[1,4,4,2,16,2048]{5,4,3,2,1,0:T(8,128)(2,1)S(1)}, bf16[1,4,4,2,16,2048]{5,4,3,2,1,0:T(8,128)(2,1)}, u32[]{:S(2)}) copy-start(bf16[1,4,4,2,16,2048]{5,4,3,2,1,0:T(8,128)(2,1)} %get-tuple-element.18) | copy-start | bytes 6291460
  273.9 2.5 copy-start.9
  273.9 2.5 copy-start.11
  279.8 2.5 copy-start.15
  332.6 13.6 %copy-start.1 = (bf16[1004,1024]{1,0:T(8,128)(2,1)S(1)}, bf16[1004,1024]{1,0:T(8,128)(2,1)}, u32[]{:S(2)}) copy-start(bf16[1004,1024]{1,0:T(8,128)(2,1)} %param.23) | copy-start | bytes 6168580

commit v3 on v2

--- a/solution.py
+++ b/solution.py
@@ -40,20 +40,6 @@
     return spread.reshape(bias_table.shape[0], length, length)
 
 
-def norm_project(rows_in, gain_vector, weights):
-    wide = rows_in.astype(F32)
-    inverse = lax.rsqrt(jnp.mean(wide * wide, axis=-1, keepdims=True) + EPSILON)
-    scaled = (wide * gain_vector).astype(BF16)
-    projected = jnp.dot(scaled, weights, preferred_element_type=F32)
-    return (projected * inverse).astype(BF16)
-
-
-def softmax_rows(scores):
-    maximum = jnp.max(scores, axis=-1, keepdims=True)
-    exponents = jnp.exp(scores - maximum)
-    return (exponents / jnp.sum(exponents, axis=-1, keepdims=True)).astype(BF16)
-
-
 def dot32(a, b, dims):
     return lax.dot_general(a, b, (dims, ((), ())), preferred_element_type=F32)
 
@@ -131,31 +117,34 @@
 
 
 class Ring:
-    def __init__(self, mover, pos, device, own, dst, units):
-        self.mover, self.pos, self.device, self.dst, self.units = mover, pos, device, dst, units
-        right, left = device(turn(pos, 1)), device(turn(pos, -1))
+    def __init__(self, mover, pos, device, own, dst, units, start=True):
+        self.mover, self.pos, self.device, self.own, self.dst = mover, pos, device, own, dst
+        self.right, self.left = device(turn(pos, 1)), device(turn(pos, -1))
         self.to_right, self.to_left = {}, {}
         half = len(units) // 2
         self.first, self.last = units[:half], units[half:]
-        for u, v in zip(units, self.last + self.first):
-            self.to_right[u] = mover.go(own(u), dst(pos, u, 1), right)
-            self.to_left[v] = mover.go(own(v), dst(pos, v, -1), left)
+        if start:
+            for u, v in zip(units, self.last + self.first):
+                self.begin_right(u)
+                self.begin_left(v)
+
+    def begin_right(self, u):
+        self.to_right[u] = self.mover.go(self.own(u), self.dst(self.pos, u, 1), self.right)
+
+    def begin_left(self, u):
+        self.to_left[u] = self.mover.go(self.own(u), self.dst(self.pos, u, -1), self.left)
 
     def onward(self):
-        right, left = self.device(turn(self.pos, 1)), self.device(turn(self.pos, -1))
+        before, after = turn(self.pos, -1), turn(self.pos, 1)
         self.far = []
         for u, v in zip(self.first, self.last):
             self.to_right[u].wait_recv()
             self.far.append(
-                self.mover.go(
-                    self.dst(turn(self.pos, -1), u, 1), self.dst(turn(self.pos, -1), u, 2), right
-                )
+                self.mover.go(self.dst(before, u, 1), self.dst(before, u, 2), self.right)
             )
             self.to_left[v].wait_recv()
             self.far.append(
-                self.mover.go(
-                    self.dst(turn(self.pos, 1), v, -1), self.dst(turn(self.pos, 1), v, 2), left
-                )
+                self.mover.go(self.dst(after, v, -1), self.dst(after, v, 2), self.left)
             )
 
     def near(self):
@@ -283,13 +272,50 @@
     )(ints)
 
 
+def norm_rows(rows, gain):
+    wide = rows.astype(F32)
+    inverse = lax.rsqrt(jnp.mean(wide * wide, axis=-1, keepdims=True) + EPSILON)
+    return (wide * gain).astype(BF16), inverse
+
+
 def fetch_kernel(
-    asked, place, memory, tok, score, live_out,
-    x_full, tokens, scores, full,
+    asked, place, memory, tok, score, live_out, w_qkv, cross_kv, cross_query,
+    live_gain, enc_gain, dec_gain,
+    x_out, tokens, scores, full, proj_mem, proj_q, qg, w_val_out,
     out_buf, in_buf0, in_buf1, own, pair_buf, a_buf, b_buf, a2_buf, b2_buf, tok_sum,
-    send, recv, a2a_send, a2a_recv, local_sem,
+    x_full, weights, acc, squares, scaled, w_query, kv_buf, w_key, w_val,
+    send, recv, a2a_send, a2a_recv, local_sem, kv_sem, out_sem,
 ):
     at = Place()
+    load_weights = [
+        pltpu.make_async_copy(w_qkv.at[i], weights.at[i], local_sem.at[i]) for i in range(3)
+    ] + [pltpu.make_async_copy(cross_query, w_query, local_sem.at[3])]
+    for copy in load_weights:
+        copy.start()
+
+    def kv_copy(i):
+        slot = lax.rem(i, 2)
+        return pltpu.make_async_copy(
+            cross_kv.at[pl.ds(i * 256, 256)], kv_buf.at[slot], kv_sem.at[slot]
+        )
+
+    kv_copy(0).start()
+
+    def split_kv(first, last):
+        def one(i, carry):
+            @pl.when(i < 15)
+            def _():
+                kv_copy(i + 1).start()
+
+            kv_copy(i).wait()
+            rows = pl.ds(pl.multiple_of(i * 256, 256), 256)
+            slot = lax.rem(i, 2)
+            w_key[rows] = kv_buf[slot, :, 0, :]
+            w_val[rows] = kv_buf[slot, :, 1, :]
+            return carry
+
+        lax.fori_loop(first, last, one, 0)
+
     greet_all(at)
     mover = Mover(send, recv)
     spread = Spread(at, mover, live_out, full, 0, 2048)
@@ -330,28 +356,52 @@
 
         lax.fori_loop(0, 32, pack, 0)
 
+    def lanes_of(pos, h):
+        return pl.ds(pl.multiple_of(pos * 1024 + h * 512, 512), 512)
+
     def part(pos, unit, k=0):
         h, g = unit
-        return x_full.at[
-            pl.ds(g * 256, 256), pl.ds(pl.multiple_of(pos * 1024 + h * 512, 512), 512)
-        ]
+        return x_full.at[pl.ds(g * 256, 256), lanes_of(pos, h)]
 
     def ring_half(h):
-        keep = pltpu.make_async_copy(
-            own.at[h], x_full.at[:, pl.ds(pl.multiple_of(at.z * 1024 + h * 512, 512), 512)],
-            local_sem.at[h],
-        )
-        keep.start()
-        ring = Ring(
+        return Ring(
             mover, at.z, at.up, lambda u: own.at[u[0], pl.ds(u[1] * 256, 256)], part,
             [(h, 0), (h, 1)],
         )
-        return ring, keep
+
+    stored = []
+
+    def multiply(k, h):
+        pos = turn(at.z, k)
+        lanes = lanes_of(pos, h)
+        if k == 0:
+            x_full[:, lanes] = own[h]
+        keep = pltpu.make_async_copy(
+            x_full.at[:, lanes], x_out.at[:, lanes], out_sem.at[len(stored)]
+        )
+        keep.start()
+        first = not stored
+        stored.append(keep)
+        gain = live_gain[:, lanes]
+        for r in range(2):
+            rows = pl.ds(r * 256, 256)
+            wide = x_full[rows, lanes].astype(F32)
+            scaled[rows] = (wide * gain).astype(BF16)
+            square = jnp.sum(wide * wide, axis=1, keepdims=True)
+            squares[rows] = square if first else squares[rows] + square
+
+        def one(i, carry):
+            product = jnp.dot(scaled[...], weights[i, lanes], preferred_element_type=F32)
+            acc[i] = product if first else acc[i] + product
+            return carry
+
+        lax.fori_loop(0, 3, one, 0)
 
     send_half(0)
     other = 1 - at.core
     pair = mover.go(tok.at[:, :, other], pair_buf, at.sibling())
     send_half(1)
+    split_kv(0, 2)
 
     pair.wait_recv()
 
@@ -379,9 +429,10 @@
     ]
     scores[at.z] = score[...]
     spread.phase_one()
+    split_kv(2, 5)
 
     wait_half(0)
-    ring0, keep0 = ring_half(0)
+    ring0 = ring_half(0)
     for copy in tok_a + tok_b:
         copy.wait_recv()
 
@@ -400,7 +451,10 @@
         for k in range(1, 4)
     ]
     wait_half(1)
-    ring1, keep1 = ring_half(1)
+    ring1 = ring_half(1)
+    for copy in load_weights:
+        copy.wait()
+    multiply(0, 0)
     for copy in tok_a2 + tok_b2:
         copy.wait_recv()
     tok_sum[:, lo] = (a2_buf[0] + a2_buf[1]) + (a2_buf[2] + a_buf[0, at.y])
@@ -412,17 +466,59 @@
     tokens[:, mine] = tok_sum[...]
     ring0.onward()
     spread.phase_one_onward()
+    multiply(0, 1)
     ring1.onward()
+    split_kv(5, 9)
     spread.phase_two()
+    ring0.near()
+    multiply(1, 0)
+    multiply(-1, 0)
+    spread.phase_two_onward()
+    split_kv(9, 16)
+    keep_values = pltpu.make_async_copy(w_val, w_val_out, local_sem.at[4])
+    keep_values.start()
     for copy in near_scores + near_tokens:
         copy.wait_recv()
-    spread.phase_two_onward()
-    for ring in (ring0, ring1):
-        ring.near()
-        ring.end()
+
+    rows, inverse = norm_rows(tokens[0:16], live_gain[...])
+
+    def project(i, carry):
+        total = jnp.dot(rows, weights[i], preferred_element_type=F32)
+        proj_q[i] = (total * inverse).astype(BF16)
+        return carry
+
+    lax.fori_loop(0, 3, project, 0)
+    rows_a, inverse_a = norm_rows(tokens[16:48], dec_gain[...])
+    queries = jnp.dot(rows_a, w_query[...], preferred_element_type=F32) * inverse_a
+    head = lax.broadcasted_iota(jnp.int32, (32, 512), 1) // HEAD
+    for h in range(8):
+        scaled[pl.ds(32 * h, 32)] = jnp.where(head == h, queries, 0.0).astype(BF16)
+
+    def fold(n, carry):
+        cols = pl.ds(pl.multiple_of(n * 1024, 1024), 1024)
+        product = dot32(scaled[pl.ds(0, 256)], w_key[cols], ((1,), (1,)))
+        qg[:, cols] = (product * enc_gain[:, cols]).astype(BF16)
+        return carry
+
+    lax.fori_loop(0, 4, fold, 0)
+    ring1.near()
+    multiply(1, 1)
+    multiply(-1, 1)
+    ring0.end()
+    multiply(2, 0)
+    ring1.end()
+    multiply(2, 1)
+    inverse_m = lax.rsqrt(squares[...] * (1.0 / 4096) + EPSILON)
+
+    def close(i, carry):
+        proj_mem[i] = (acc[i] * inverse_m).astype(BF16)
+        return carry
+
+    lax.fori_loop(0, 3, close, 0)
     spread.finish()
-    keep0.wait()
-    keep1.wait()
+    for copy in stored:
+        copy.wait()
+    keep_values.wait()
     mover.finish_sends()
 
     def sent(d, carry):
@@ -433,7 +529,7 @@
     lax.fori_loop(1, 32, sent, 0)
 
 
-def fetch(asked, place, memory, tok, score, live_out):
+def fetch(*args):
     return pl.pallas_call(
         fetch_kernel,
         out_shape=(
@@ -441,9 +537,13 @@
             jax.ShapeDtypeStruct((48, 4096), BF16),
             jax.ShapeDtypeStruct((4, 1, 128), F32),
             jax.ShapeDtypeStruct((3, 4, 4, 2, 16, 2048), BF16),
+            jax.ShapeDtypeStruct((3, 512, 512), BF16),
+            jax.ShapeDtypeStruct((3, 16, 512), BF16),
+            jax.ShapeDtypeStruct((256, 4096), BF16),
+            jax.ShapeDtypeStruct((4096, 512), BF16),
         ),
-        in_specs=[SM, SM, VM, VM, VM, ANY],
-        out_specs=(ANY, VM, VM, ANY),
+        in_specs=[SM, SM, VM, VM, VM, ANY, ANY, ANY, ANY, VM, VM, VM],
+        out_specs=(ANY, VM, VM, ANY, VM, VM, VM, ANY),
         scratch_shapes=[
             pltpu.VMEM((2, 64, 16, 512), BF16), pltpu.VMEM((64, 16, 512), BF16),
             pltpu.VMEM((64, 16, 512), BF16),
@@ -451,108 +551,284 @@
             pltpu.VMEM((3, 4, 48, 512), BF16), pltpu.VMEM((3, 4, 48, 512), BF16),
             pltpu.VMEM((3, 48, 512), BF16), pltpu.VMEM((3, 48, 512), BF16),
             pltpu.VMEM((48, 1024), BF16),
+            pltpu.VMEM((512, 4096), BF16), pltpu.VMEM((3, 4096, 512), BF16),
+            pltpu.VMEM((3, 512, 512), F32), pltpu.VMEM((512, 1), F32),
+            pltpu.VMEM((512, 512), BF16), pltpu.VMEM((4096, 512), BF16),
+            pltpu.VMEM((2, 256, 2, 512), BF16), pltpu.VMEM((4096, 512), BF16),
+            pltpu.VMEM((4096, 512), BF16),
             pltpu.SemaphoreType.DMA((80,)), pltpu.SemaphoreType.DMA((80,)),
             pltpu.SemaphoreType.DMA((2, 32)), pltpu.SemaphoreType.DMA((2, 32)),
-            pltpu.SemaphoreType.DMA((2,)),
+            pltpu.SemaphoreType.DMA((5,)), pltpu.SemaphoreType.DMA((2,)),
+            pltpu.SemaphoreType.DMA((8,)),
         ],
-        compiler_params=params(2, 40),
-    )(asked, place, memory, tok, score, live_out)
-
-
-def context_kernel(ctx, live_out, others, full, send, recv):
+        compiler_params=params(2, 60),
+    )(*args)
+
+
+def reader_kernel(
+    proj_mem, proj_q, bias, x_mem, tokens, qg, scores, left_in, live_out, w_val_in, cross_out_in,
+    enc_gain,
+    encoded, decoded,
+    ctx, others, x_seq, left, right, own_out, w_val, w_out, ql, ql_part, s, w, zc, zed, heads_out,
+    inv, parts, part_buf, send, recv, local_sem,
+):
     at = Place()
+    loads = [
+        pltpu.make_async_copy(a, b, local_sem.at[i])
+        for i, (a, b) in enumerate([
+            (x_mem, x_seq.at[:, pl.ds(0, 16)]), (live_out, own_out), (left_in, left),
+            (w_val_in, w_val), (cross_out_in, w_out),
+        ])
+    ]
+    for copy in loads:
+        copy.start()
     greet_all(at)
     mover = Mover(send, recv)
-    spread = Spread(at, mover, live_out, full, 2048, 2048)
-    rows = lambda u: pl.ds(u * 256, 256)
+    spread = Spread(at, mover, live_out, right, 2048, 2048)
+    scale = HEAD ** (-0.5)
+    nt = ((1,), (1,))
+
+    def chunk(j):
+        return pl.ds(pl.multiple_of(j * 256, 256), 256)
 
     def part(pos, u, k):
-        return others.at[{1: 2, -1: 0, 2: 1}[k], rows(u)]
-
-    ring = Ring(mover, at.z, at.up, lambda u: ctx.at[rows(u)], part, [0, 1, 2, 3])
-    spread.phase_one()
+        return others.at[{1: 2, -1: 0, 2: 1}[k], chunk(turn(pos, u))]
+
+    ring = Ring(
+        mover, at.z, at.up, lambda u: ctx.at[chunk(turn(at.z, u))], part, [1, 2, 3, 0], False
+    )
+
+    low = lax.broadcasted_iota(jnp.int32, (128, 128), 1) < HEAD
+
+    def attend(j):
+        def group(g, carry):
+            first = j * 8 + g * 4
+
+            def pair(i, p):
+                lanes = pl.ds(128 * p, 128)
+                pieces = []
+                for n in range(4):
+                    pieces.append(
+                        proj_mem[i, pl.ds(pl.multiple_of((first + n) * 16, 16), 16), lanes]
+                    )
+                    pieces.append(proj_q[i, :, lanes])
+                return jnp.concatenate(pieces, axis=0)
+
+            for p in range(4):
+                q, k, v = pair(0, p), pair(1, p), pair(2, p)
+                both = []
+                for e in range(2):
+                    keep = low if e == 0 else jnp.logical_not(low)
+                    sc = dot32(jnp.where(keep, q, jnp.zeros_like(q)), k, nt) * scale
+                    sc = sc + bias[2 * p + e]
+                    ex = jnp.exp(sc - jnp.max(sc, axis=1, keepdims=True))
+                    ex = (ex / jnp.sum(ex, axis=1, keepdims=True)).astype(BF16)
+                    both.append(jnp.dot(ex, v, preferred_element_type=F32))
+                ctx[pl.ds(pl.multiple_of(first * 32, 128), 128), pl.ds(128 * p, 128)] = jnp.where(
+                    low, both[0], both[1]
+                ).astype(BF16)
+            return carry
+
+        lax.fori_loop(0, 2, group, 0)
+
+    for n, u in enumerate((1, 3, 2, 0)):
+        attend(turn(at.z, u))
+        ring.begin_right(u)
+        ring.begin_left(u)
+        if n == 0:
+            spread.phase_one()
+
+    loads[0].wait()
+
+    def fill(p, carry):
+        x_seq[p, pl.ds(16, 16)] = tokens[pl.ds(0, 16)]
+        return carry
+
+    lax.fori_loop(0, 32, fill, 0)
     spread.phase_one_onward()
+
+    def rows_of(j):
+        return x_seq[pl.ds(j * 8, 8)].reshape(256, 4096)
+
+    def score_inputs(j, carry):
+        s[j] = dot32(qg[...], rows_of(j), nt)
+        return carry
+
+    lax.fori_loop(0, 4, score_inputs, 0)
     ring.onward()
+    loads[1].wait()
+    ql[0] = dot32(qg[...], own_out[...], nt).astype(BF16)
+
+    def score_own(j, carry):
+        s[j] = s[j] + dot32(ql[0], ctx[chunk(j)], nt)
+        return carry
+
+    lax.fori_loop(0, 4, score_own, 0)
     spread.phase_two()
+    mine = chunk(at.z)
+
+    def attend_own(n, carry):
+        cols = pl.ds(pl.multiple_of(n * 1024, 1024), 1024)
+        zed[:, cols] = (
+            jnp.dot(ctx[mine], own_out[:, cols], preferred_element_type=F32)
+            .astype(BF16).astype(F32)
+        )
+        return carry
+
+    lax.fori_loop(0, 4, attend_own, 0)
+    loads[2].wait()
+
+    def fold_left(k, carry):
+        ql_part[k] = dot32(qg[:, pl.ds(0, 2048)], left[k], nt)
+        return carry
+
+    lax.fori_loop(0, 3, fold_left, 0)
     spread.phase_two_onward()
     ring.near()
     ring.end()
+
+    def group_rows(k, n):
+        if n < 2:
+            return left[k, :, pl.ds(n * 1024, 1024)]
+        return right[k, :, :, :, :, pl.ds((n - 2) * 1024, 1024)].reshape(512, 1024)
+
+    def attend_other(n):
+        def one(k, carry):
+            cols = pl.ds(n * 1024, 1024)
+            zed[:, cols] = zed[:, cols] + (
+                jnp.dot(others[k, mine], group_rows(k, n), preferred_element_type=F32)
+                .astype(BF16).astype(F32)
+            )
+            return carry
+
+        lax.fori_loop(0, 3, one, 0)
+
+    attend_other(0)
+    attend_other(1)
     spread.finish()
-    mover.finish_sends()
-
-
-def share_context(ctx, live_out):
-    return pl.pallas_call(
-        context_kernel,
-        out_shape=(
-            jax.ShapeDtypeStruct((3, 1024, 512), BF16),
-            jax.ShapeDtypeStruct((3, 4, 4, 2, 16, 2048), BF16),
-        ),
-        in_specs=[ANY, ANY],
-        out_specs=(ANY, ANY),
-        scratch_shapes=[pltpu.SemaphoreType.DMA((64,)), pltpu.SemaphoreType.DMA((64,))],
-        compiler_params=params(3, 8),
-    )(ctx, live_out)
-
-
-def greet_z(at):
-    barrier = pltpu.get_barrier_semaphore()
-    for k in range(1, 4):
-        pl.semaphore_signal(barrier, inc=1, device_id=at.up(turn(at.z, k)), device_id_type=MESH)
-    pl.semaphore_wait(barrier, 3)
-
-
-def inverse_kernel(mine, every, send, recv):
-    at = Place()
-    every[at.z] = mine[...]
-    greet_z(at)
-    mover = Mover(send, recv)
-    near = [mover.go(mine, every.at[at.z], at.up(turn(at.z, k))) for k in range(1, 4)]
+    attend_other(2)
+    attend_other(3)
+
+    own_rows = rows_of(at.z).astype(F32) + zed[...]
+    own_rows = own_rows.astype(BF16)
+    encoded[...] = own_rows
+    own_rows = own_rows.astype(F32)
+    norm = lax.rsqrt(jnp.sum(own_rows * own_rows, axis=1, keepdims=True) * (1.0 / 4096) + EPSILON)
+    inv[at.z] = jnp.transpose(jnp.broadcast_to(norm, (256, 128)))[0:1]
+    near = [mover.go(inv.at[at.z], inv.at[at.z], at.up(turn(at.z, k))) for k in range(1, 4)]
+
+    def fold_right(k, carry):
+        ql[k + 1] = (
+            ql_part[k] + dot32(qg[:, pl.ds(2048, 2048)], right[k].reshape(512, 2048), nt)
+        ).astype(BF16)
+        return carry
+
+    lax.fori_loop(0, 3, fold_right, 0)
+
+    def score_others(j, carry):
+        total = s[j]
+        for k in range(3):
+            total = total + dot32(ql[k + 1], others[k, chunk(j)], nt)
+        s[j] = total
+        return carry
+
+    lax.fori_loop(0, 4, score_others, 0)
     for copy in near:
         copy.wait_recv()
-    mover.finish_sends()
-
-
-def share_inverse(mine):
-    return pl.pallas_call(
-        inverse_kernel,
-        out_shape=jax.ShapeDtypeStruct((4, 2, 128), F32),
-        in_specs=[VM],
-        out_specs=VM,
-        scratch_shapes=[pltpu.SemaphoreType.DMA((4,)), pltpu.SemaphoreType.DMA((4,))],
-        compiler_params=params(4, 4),
-    )(mine)
-
-
-def decoded_kernel(part, out, buf, send, recv):
-    at = Place()
-    greet_z(at)
-    mover = Mover(send, recv)
-    near = [
-        mover.go(part.at[turn(at.z, k)], buf.at[k - 1], at.up(turn(at.z, k)))
+
+    passage = lax.broadcasted_iota(jnp.int32, (1, 256), 1) // 32
+    top = None
+    for j in range(4):
+        row = jnp.zeros((1, 256), F32)
+        line = scores[j]
+        for p in range(8):
+            row = row + jnp.where(passage == p, line[:, p : p + 1], 0.0)
+        total = s[j] * (inv[j] * scale) + row
+        s[j] = total
+        here = jnp.max(total, axis=1, keepdims=True)
+        top = here if top is None else jnp.maximum(top, here)
+    sums = jnp.zeros((256, 1), F32)
+    for j in range(4):
+        ex = jnp.exp(s[j] - top)
+        s[j] = ex
+        sums = sums + jnp.sum(ex, axis=1, keepdims=True)
+    for j in range(4):
+        w[j] = (s[j] * inv[j] / sums).astype(BF16)
+
+    def mix(source):
+        total = jnp.zeros((256, 512), F32)
+        for j in range(4):
+            total = total + jnp.dot(w[j], source[pl.ds(256 * j, 256)], preferred_element_type=F32)
+        return total.astype(BF16)
+
+    zc[0] = mix(ctx)
+
+    def mix_other(k, carry):
+        zc[k + 1] = mix(others.at[k])
+        return carry
+
+    lax.fori_loop(0, 3, mix_other, 0)
+    for copy in loads[3:]:
+        copy.wait()
+    for n in range(4):
+        cols = pl.ds(n * 1024, 1024)
+        total = jnp.dot(zc[0], own_out[:, cols], preferred_element_type=F32)
+        for j in range(4):
+            total = total + jnp.dot(
+                w[j], x_seq[pl.ds(8 * j, 8), :, cols].reshape(256, 1024),
+                preferred_element_type=F32,
+            )
+        for k in range(3):
+            total = total + jnp.dot(zc[k + 1], group_rows(k, n), preferred_element_type=F32)
+        total = (total * enc_gain[:, cols]).astype(BF16)
+        product = jnp.dot(total, w_val[cols], preferred_element_type=F32)
+        heads_out[...] = product if n == 0 else heads_out[...] + product
+    head = lax.broadcasted_iota(jnp.int32, (32, 512), 1) // HEAD
+    context = jnp.zeros((32, 512), F32)
+    for h in range(8):
+        context = context + jnp.where(head == h, heads_out[pl.ds(32 * h, 32)], 0.0)
+    context = context.astype(BF16)
+    for j in range(4):
+        parts[j] = jnp.dot(
+            context, w_out[:, pl.ds(1024 * j, 1024)], preferred_element_type=F32
+        ).astype(BF16)
+    last = [
+        mover.go(parts.at[turn(at.z, k)], part_buf.at[k - 1], at.up(turn(at.z, k)))
         for k in range(1, 4)
     ]
-    for copy in near:
+    for copy in last:
         copy.wait_recv()
-    total = part[at.z].astype(F32)
+    total = parts[at.z].astype(F32)
     for k in range(3):
-        total = total + buf[k].astype(F32)
-    out[...] = total.astype(BF16)
+        total = total + part_buf[k].astype(F32)
+    decoded[...] = total.astype(BF16)
     mover.finish_sends()
 
 
-def add_decoded(part):
+def reader(*args):
     return pl.pallas_call(
-        decoded_kernel,
-        out_shape=jax.ShapeDtypeStruct((32, 1024), BF16),
-        in_specs=[VM],
-        out_specs=VM,
+        reader_kernel,
+        out_shape=(
+            jax.ShapeDtypeStruct((256, 4096), BF16),
+            jax.ShapeDtypeStruct((32, 1024), BF16),
+        ),
+        in_specs=[VM, VM, VM, ANY, VM, VM, VM, ANY, ANY, ANY, ANY, VM],
+        out_specs=(VM, VM),
         scratch_shapes=[
-            pltpu.VMEM((3, 32, 1024), BF16),
-            pltpu.SemaphoreType.DMA((4,)), pltpu.SemaphoreType.DMA((4,)),
+            pltpu.VMEM((1024, 512), BF16), pltpu.VMEM((3, 1024, 512), BF16),
+            pltpu.VMEM((32, 32, 4096), BF16), pltpu.VMEM((3, 512, 2048), BF16),
+            pltpu.VMEM((3, 4, 4, 2, 16, 2048), BF16), pltpu.VMEM((512, 4096), BF16),
+            pltpu.VMEM((4096, 512), BF16), pltpu.VMEM((512, 4096), BF16),
+            pltpu.VMEM((4, 256, 512), BF16), pltpu.VMEM((3, 256, 512), F32),
+            pltpu.VMEM((4, 256, 256), F32), pltpu.VMEM((4, 256, 256), BF16),
+            pltpu.VMEM((4, 256, 512), BF16), pltpu.VMEM((256, 4096), F32),
+            pltpu.VMEM((256, 512), F32), pltpu.VMEM((4, 1, 256), F32),
+            pltpu.VMEM((4, 32, 1024), BF16), pltpu.VMEM((3, 32, 1024), BF16),
+            pltpu.SemaphoreType.DMA((64,)), pltpu.SemaphoreType.DMA((64,)),
+            pltpu.SemaphoreType.DMA((5,)),
         ],
-        compiler_params=params(5, 8),
-    )(part)
+        compiler_params=params(3, 60),
+    )(*args)
 
 
 def shards(
@@ -562,7 +838,6 @@
     n_cache = lax.axis_size("cache")
     n_psg = lax.axis_size("psg")
     me_c = lax.axis_index("cache")
-    me_z = lax.axis_index("psg")
     width = live_gain.shape[0]
     plen = memory.shape[1]
     qlen = question_ids.shape[1]
@@ -570,9 +845,7 @@
     own_count = owner.shape[1]
     total = own_count * n_psg
     seq = plen + qlen
-    heads = rel_bias.shape[0]
     cols = live_out.shape[0]
-    scale = HEAD ** (-0.5)
 
     ints = jnp.concatenate(
         [question_ids[0], answer_ids[0], owner[0, :, 0], slot[0], jnp.zeros((64,), jnp.int32)]
@@ -597,84 +870,21 @@
     ).astype(BF16)
     tok = jnp.einsum("qtv,vf->qtf", onehot, embedding, preferred_element_type=F32).astype(BF16)
     score = jnp.pad(passage_score, ((0, 0), (0, 120)))
-    x_mem, token_full, scores, full_left = fetch(
-        asked, place, memory, tok.reshape(4, 4, 2, qlen + alen, -1), score, live_out
+    x_mem, token_full, scores, full_left, proj_mem, proj_q, qg, w_val = fetch(
+        asked, place, memory, tok.reshape(4, 4, 2, qlen + alen, -1), score, live_out,
+        jnp.transpose(live_qkv, (1, 0, 2)), cross_kv, cross_query,
+        live_gain.reshape(1, width), enc_gain.reshape(1, width), dec_gain.reshape(1, width),
     )
-    x_q = token_full[:qlen]
-    answer = token_full[qlen:]
-    score_all = scores[:, 0, :own_count].reshape(total)
-
-    q_dec = norm_project(answer, dec_gain, cross_query).reshape(alen, heads, HEAD)
-    kv = cross_kv.reshape(width, 2 * cols)
-    w_key = kv[:, :cols].reshape(width, heads, HEAD)
-    w_val = kv[:, cols:].reshape(width, heads, HEAD)
-    qg = (
-        jnp.einsum("thd,fhd->htf", q_dec, w_key, preferred_element_type=F32) * enc_gain
-    ).astype(BF16).reshape(heads * alen, width)
-
-    proj = []
-    for i in range(3):
-        w = live_qkv[:, i]
-        m = norm_project(x_mem, live_gain, w).reshape(total, plen, cols)
-        n = norm_project(x_q, live_gain, w)
-        proj.append(
-            jnp.concatenate([m, jnp.broadcast_to(n[None], (total, qlen, cols))], axis=1).reshape(
-                total, seq, heads, HEAD
-            )
-        )
-    scores = jnp.einsum(
-        "pqhd,pkhd->phqk", proj[0], proj[1], preferred_element_type=F32
-    ) * scale + position_bias(rel_bias, seq)[None]
-    ctx = (
-        jnp.einsum("phqk,pkhd->pqhd", softmax_rows(scores), proj[2],
-                   preferred_element_type=F32)
-        .astype(BF16).reshape(total * seq, cols)
+    position = position_bias(rel_bias, seq)
+    block = np.arange(128) // seq
+    bias = jnp.where(
+        jnp.asarray(block[:, None] == block[None, :])[None], jnp.tile(position, (1, 4, 4)), -1e30
     )
-    others, full_right = share_context(ctx, live_out)
-    ctx_all = [ctx] + [others[k] for k in range(3)]
-    full_left = full_left.reshape(3, cols, width // 2)
-    full_right = full_right.reshape(3, cols, width // 2)
-    out_full = [live_out] + [
-        jnp.concatenate([full_left[k], full_right[k]], axis=1) for k in range(3)
-    ]
-    ql = [dot32(qg, o, ((1,), (1,))).astype(BF16) for o in out_full]
-
-    own_rows = own_count * seq
-    own_ctx = [lax.dynamic_slice_in_dim(c, me_z * own_rows, own_rows, 0) for c in ctx_all]
-    attended = sum(
-        dot32(own_ctx[z], out_full[z], ((1,), (0,))).astype(BF16).astype(F32) for z in range(n_psg)
+    encoded, decoded = reader(
+        proj_mem, proj_q, bias, x_mem.reshape(total, plen, width), token_full, qg, scores,
+        full_left.reshape(3, cols, width // 2), live_out, w_val, cross_out,
+        enc_gain.reshape(1, width),
     )
-    own_mem = lax.dynamic_slice_in_dim(x_mem, me_z * own_count * plen, own_count * plen, 0)
-    own_input = jnp.concatenate(
-        [own_mem.reshape(own_count, plen, width),
-         jnp.broadcast_to(x_q[None], (own_count, qlen, width))], axis=1,
-    ).reshape(own_rows, width)
-    encoded = (own_input.astype(F32) + attended).astype(BF16)
-    enc32 = encoded.astype(F32)
-    inv_own = lax.rsqrt(jnp.mean(enc32 * enc32, axis=-1) + EPSILON)
-    inv = share_inverse(inv_own.reshape(2, 128)).reshape(total * seq)
-
-    s_mem = dot32(qg, x_mem, ((1,), (1,))).reshape(-1, total, plen)
-    s_q = jnp.broadcast_to(dot32(qg, x_q, ((1,), (1,)))[:, None], (heads * alen, total, qlen))
-    s = jnp.concatenate([s_mem, s_q], axis=2).reshape(heads * alen, total * seq)
-    for z in range(n_psg):
-        s = s + dot32(ql[z], ctx_all[z], ((1,), (1,)))
-    s = s * (inv * scale)[None] + jnp.repeat(score_all, seq)[None]
-    top = jnp.max(s, axis=-1, keepdims=True)
-    e = jnp.exp(s - top)
-    sums = jnp.sum(e, axis=-1, keepdims=True)
-    w = (e * inv[None] / sums).astype(BF16)
-    w3 = w.reshape(-1, total, seq)
-    w_mem = w3[:, :, :plen].reshape(-1, total * plen)
-    w_q = jnp.sum(w3[:, :, plen:].astype(F32), axis=1).astype(BF16)
-    zed = dot32(w_mem, x_mem, ((1,), (0,))) + dot32(w_q, x_q, ((1,), (0,)))
-    for z in range(n_psg):
-        part = dot32(w, ctx_all[z], ((1,), (0,))).astype(BF16)
-        zed = zed + dot32(part, out_full[z], ((1,), (0,)))
-    zed = (zed * enc_gain).astype(BF16).reshape(heads, alen, width)
-    context = jnp.einsum("htf,fhd->thd", zed, w_val, preferred_element_type=F32).astype(BF16)
-    part = dot32(context.reshape(alen, -1), cross_out, ((1,), (0,))).astype(BF16)
-    decoded = add_decoded(part.reshape(alen, n_psg, -1).transpose(1, 0, 2))
     return encoded.reshape(1, own_count, seq, width), decoded[None]
 
 

time: 353 us -> 211 us (0.60); the launches traced: 346 us -> 211 us
  matrix products: 120 us -> 5.04 us
  local copies, waits for them, and re-layouts: 64.2 us -> 10.9 us
  Pallas kernels: 147 us -> 192 us
  other arithmetic: 13 us -> 2.31 us
    dot_general x28 -> x0, matrix products: 116 us -> none  [the longest x17 78.3 us: dot32(): return lax.dot_general(a, b, (dims, ((), ())), preferred_element_type=F32)]
    reshape x6 -> x0, local copies, waits for them, and re-layouts: 26.1 us -> none  [the longest x1 21.2 us: shards(): kv = cross_kv.reshape(width, 2 * cols)]
    pallas_call x3 -> x1, Pallas kernels: 55.6 us -> 80.7 us  [reader(): pl.pallas_call(reader_kernel, out_shape=(jax.ShapeDtypeStruct((256, 4096)...]
    pallas_call x1, Pallas kernels: 74.7 us -> 93.9 us  [fetch(): pl.pallas_call(fetch_kernel, out_shape=(jax.ShapeDtypeStruct((512, 4096),...]
    slice x6 -> x0, local copies, waits for them, and re-layouts: 15.2 us -> none  [the longest x1 5.43 us: shards(): w_val = kv[:, cols:].reshape(width, heads, HEAD)]
    sub x1 -> x0, other arithmetic: 7.07 us -> none  [softmax_rows(): exponents = jnp.exp(scores - maximum)]
    unnamed x53 -> x14, local copies, waits for them, and re-layouts: 10.5 us -> 3.82 us
    another operation x1 -> x3, local copies, waits for them, and re-layouts: 0.09 us -> 4.32 us  [shards(): jnp.tile(position, (1, 4, 4))]
where the time goes in v3:
time: 211 us
  Pallas kernels  192 us (91%)
  local copies, waits for them, and re-layouts  10.9 us (5%)
  matrix products  5.04 us (2%)
  other arithmetic  2.31 us (1%)
    pallas_call x1, Pallas kernels, fetch(): pl.pallas_call(fetch_kernel, out_shape=(jax.ShapeDtypeStruct((512, 4096),...  93.9 us
    pallas_call x1, Pallas kernels, reader(): pl.pallas_call(reader_kernel, out_shape=(jax.ShapeDtypeStruct((256, 4096)...  80.7 us
    pallas_call x1, Pallas kernels, index_exchange(): pl.pallas_call(index_kernel, out_shape=jax.ShapeDtypeStruct((32, 4, 1, 12...  16.9 us
    dot_general x1, matrix products, shards(): jnp.einsum('qtv,vf->qtf', onehot, embedding, preferred_element_type=F32)  4.85 us
    another operation x3, local copies, waits for them, and re-layouts, shards(): jnp.tile(position, (1, 4, 4))  4.32 us

profile of v3, /device:TPU:1, one launch (start us, length us, event | category | flops | bytes accessed | tf_op | source)
XLA Modules:
  0.0 210.6 jit_solution(7084167325766897914)
XLA Ops:
  0.6 0.0 copy-start
  0.7 0.9 concatenate.3
  1.6 16.9 %shard_map.185 = s32[32,4,1,128]{3,2,1,0:T(1,128)S(1)} custom-call(s32[1,128]{1,0:T(1,128)S(1)} %bitcast.31), custom_call_target="tpu_custom_call" | custom-call | tf_op jit(solution)/shard_map/pallas_call | solution.py:262
  18.5 0.1 fusion.6
  18.7 0.1 copy.34
  18.8 0.1 copy.36
  18.9 0.8 convert_reduce_fusion
  19.6 0.5 fusion.5.place
  20.2 0.1 copy.35
  20.3 0.1 copy.38
  20.3 0.1 copy.39
  20.4 0.1 select_reduce_fusion
  20.5 0.1 copy.40
  20.6 0.6 reshape.74.asked
  21.3 0.0 copy-done
  21.3 0.0 copy-start.5
  21.3 4.9 %fusion.2 = bf16[32,48,1024]{2,1,0:T(8,128)(2,1)} fusion(s32[32,48]{1,0:T(8,128)S(1)} %bitcast.45, bf16[1004,1024]{1,0:T(8,128)(2,1)S(1)} %copy-done), kind=kOutput, calls=%fused_computation.3 | convolution fusion | flops 3161425920 | bytes 5208064 | tf_op jit(solution)/shard_map/qtv,vf->qtf/dot_general | solution.py:871
  26.2 0.0 copy-done.5
  26.2 0.6 pad.4.score
  26.7 0.0 copy-start.1
  26.7 0.0 copy-start.4
  26.7 93.9 %shard_map.186 = (bf16[512,4096]{1,0:T(8,128)(2,1)}, bf16[48,4096]{1,0:T(8,128)(2,1)}, f32[4,1,128]{2,1,0:T(1,128)}, bf16[3,4,4,2,16,2048]{5,4,3,2,1,0:T(8,128)(...) custom-call(s32[64]{0:T(128)} %reshape.74.asked, ...), custom_call_target="tpu_custom_call" | custom-call | tf_op jit(solution)/shard_map/pallas_call | solution.py:533
  120.7 0.0 copy-start.3
  120.7 0.0 copy-done.1
  120.7 0.0 copy-done.4
  120.7 0.2 convolution_bitcast_fusion
  120.9 0.1 tile.10
  121.0 1.8 tile.11
  122.8 2.4 %tile.12 = f32[8,128,128]{2,1,0:T(8,128)S(1)} reshape(f32[8,4,32,4,32]{4,3,2,1,0:T(4,128)} %tile.11) | data formatting | bytes 1048576 | tf_op jit(solution)/shard_map/tile | solution.py:881
  125.2 0.0 copy-done.3
  125.2 0.8 broadcast_select_fusion.bias
  126.1 80.7 %shard_map.187 = (bf16[256,4096]{1,0:T(8,128)(2,1)}, bf16[32,1024]{1,0:T(8,128)(2,1)}) custom-call(bf16[3,512,512]{2,1,0:T(8,128)(2,1)} %get-tuple-element.12.proj_mem, bf16[3,16,512]{2,1,0:T(8,128)(2,1)} %get-tuple-element.13.proj_q, f32[8,128,128]{2,1,0:T(8,128)} %broadcast_select_fusion.bias, bf16[32,16,4096]{2,1,0:T(8,128)(2,1)} %bitcast.34, ...), custom_call_target="tpu_custom_call" | custom-call | tf_op jit(solution)/shard_map/pallas_call | solution.py:809
  206.8 0.0 copy-start.2
  206.8 3.2 %copy.44 = bf16[1,8,32,4096]{3,2,1,0:T(8,128)(2,1)} copy(bf16[1,8,32,4096]{3,2,1,0:T(8,128)(2,1)} %bitcast.36) | data formatting | bytes 4194304
  209.9 0.0 copy-done.2
  209.9 0.6 copy.45
  (4 shorter events, 0.0 us)
Async XLA Ops:
  0.6 20.7 %copy-start = (bf16[1004,1024]{1,0:T(8,128)(2,1)S(1)}, bf16[1004,1024]{1,0:T(8,128)(2,1)}, u32[]{:S(2)}) copy-start(bf16[1004,1024]{1,0:T(8,128)(2,1)} %param.24) | copy-start | bytes 6168580
  21.3 4.9 %copy-start.5 = (f32[1,8]{1,0:T(1,128)S(1)}, f32[1,8]{1,0:T(1,128)}, u32[]{:S(2)}) copy-start(f32[1,8]{1,0:T(1,128)} %param.22) | copy-start | bytes 100
  26.7 94.0 %copy-start.1 = (f32[32,1024]{1,0:T(8,128)S(1)}, f32[32,1024]{1,0:T(8,128)}, u32[]{:S(2)}) copy-start(f32[32,1024]{1,0:T(8,128)} %constant.26.clone) | copy-start | bytes 393220
  26.7 94.0 %copy-start.4 = (f32[8,32]{1,0:T(8,128)S(1)}, f32[8,32]{1,0:T(8,128)}, u32[]{:S(2)}) copy-start(f32[8,32]{1,0:T(8,128)} %param.27) | copy-start | bytes 3076
  120.7 4.6 %copy-start.3 = (pred[128,128]{1,0:T(32,128)(4,1)S(1)}, pred[128,128]{1,0:T(32,128)(4,1)}, u32[]{:S(2)}) copy-start(pred[128,128]{1,0:T(32,128)(4,1)} %constant.27.clone) | copy-start | bytes 49156
  206.8 3.2 %copy-start.2 = (bf16[32,1024]{1,0:T(8,128)(2,1)S(1)}, bf16[32,1024]{1,0:T(8,128)(2,1)}, u32[]{:S(2)}) copy-start(bf16[32,1024]{1,0:T(8,128)(2,1)} %get-tuple-element.21) | copy-start | bytes 196612
